TPU v7x, 32 devices: a whole 2x2x4 slice. The times are simulated.
32 devices in a mesh: ens: 2 (over y), row: 4 (over z), col: 4 (over x, core).
Axes of the slice: x: 2, y: 2, z: 4, core: 2. Of those that a mesh axis runs over, the one named last changes fastest.
Arguments:
- series: float32 [24576, 256], P(('ens', 'row', 'col')), parts along dimension 0, may hold values from -22 to 22, as said below
- vectors: float32 [24576, 128], P(('ens', 'row', 'col')), parts along dimension 0, may hold values from -6 to 6
- damp_class: int32 [24576], P(('ens', 'row', 'col')), parts along dimension 0, may hold values from 0 to 15
- damp_levels: float32 [16], replicated, may hold values from 0.5 to 2
- removed_blocks: int32 [64, 32], P('ens'), parts along dimension 0, may hold values 0 or 1
Outputs:
- filtered: float32 [24576, 128], P(('ens', 'row', 'col')), parts along dimension 0
There are 2 independent parts, one for each index of `ens`. A program takes and returns all parts, laid end to end along the dimension named above; an argument that names none is the same for every part. Nothing has to cross between parts.
Inputs may be any that keep to these rules, and one draw needn't show every extreme that they name: Each voxel's series is not constant.
All inputs are finite; a program needn't handle non-finite values.
Results may differ from a plain program's by a relative error of at most 0.0003.
Values sent between devices are 32-bit elements; how exact they have to be, the bound alone decides.
A program may use at most 128 MiB of HBM per device.

v0:
```python
import jax
import jax.numpy as jnp
from jax import lax
from jax.sharding import PartitionSpec as P

N = 12288


sharpness = 12.0


def standardize(series):
    centered = series - jnp.mean(series, axis=1, keepdims=True)
    spread = jnp.mean(centered * centered, axis=1, keepdims=True)
    return centered * lax.rsqrt(spread + 1e-05)


def local(series, vectors, damp_class, damp_levels, removed_blocks):
    n_col = lax.axis_size("col")
    row_id = lax.axis_index("row")
    col_id = lax.axis_index("col")
    shard_rows = series.shape[0]
    samples = series.shape[1]
    classes = damp_levels.shape[0]
    z_own = standardize(series)
    onehot = (damp_class[:, None] == jnp.arange(classes, dtype=jnp.int32)[None, :]).astype(
        jnp.float32
    )
    damping = jnp.sum(onehot * damp_levels[None, :], axis=1)
    z_rows, d_rows = (
        lax.all_gather(z_own, "col", axis=0, tiled=True),
        lax.all_gather(damping, "col", axis=0, tiled=True),
    )
    tile_rows = z_rows.shape[0]
    blocks = removed_blocks.shape[0]
    block_size = N // blocks
    row_blocks = tile_rows // block_size
    keep_rows = 1.0 - lax.dynamic_slice_in_dim(
        removed_blocks, row_id * row_blocks, row_blocks, 0
    ).astype(jnp.float32)
    shard_piece = lax.all_gather(z_own, "row", axis=0, tiled=True)
    count = shard_piece.shape[0]
    position = jnp.arange(count, dtype=jnp.int32)
    owner_row = position // shard_rows
    global_index = (owner_row * n_col + col_id) * shard_rows + position % shard_rows
    col_block = global_index // block_size
    onehot_cols = (col_block[None, :] == jnp.arange(blocks, dtype=jnp.int32)[:, None]).astype(
        jnp.float32
    )
    keep_small = jnp.dot(
        keep_rows, onehot_cols, precision=lax.Precision.HIGHEST, preferred_element_type=jnp.float32
    )
    keep_full = jnp.broadcast_to(keep_small[:, None, :], (row_blocks, block_size, count)).reshape(
        tile_rows, count
    )
    correlation = (
        lax.dot_general(
            z_rows,
            shard_piece,
            (((1,), (1,)), ((), ())),
            precision=lax.Precision.HIGHEST,
            preferred_element_type=jnp.float32,
        )
        / samples
    )
    affinity = jnp.tanh(sharpness * correlation) * keep_full * d_rows[:, None]
    spectral_scale = 0.5 * N * jnp.mean(damp_levels * damp_levels)

    def forward_add(shard_piece):
        return jnp.dot(
            affinity,
            shard_piece,
            precision=lax.Precision.HIGHEST,
            preferred_element_type=jnp.float32,
        )

    def backward_add(shard_piece):
        return lax.dot_general(
            affinity,
            shard_piece,
            (((0,), (0,)), ((), ())),
            precision=lax.Precision.HIGHEST,
            preferred_element_type=jnp.float32,
        )

    def normal_apply(field_in):
        product = forward_add(lax.all_gather(field_in, "row", axis=0, tiled=True))
        product = lax.psum_scatter(product, "col", scatter_dimension=0, tiled=True)
        returned = backward_add(lax.all_gather(product, "col", axis=0, tiled=True))
        return lax.psum_scatter(returned, "row", scatter_dimension=0, tiled=True) / spectral_scale

    first_term = normal_apply(vectors) - vectors
    filtered = 2.0 * (normal_apply(first_term) - first_term) - vectors
    return filtered


def solution(mesh):
    placed = (
        P(("ens", "row", "col"), None),
        P(("ens", "row", "col"), None),
        P(("ens", "row", "col")),
        P(),
        P("ens", None),
    )
    return jax.shard_map(
        local, mesh=mesh, in_specs=placed, out_specs=P(("ens", "row", "col"), None), check_vma=False
    )
```

profile of v0, /device:TPU:0, one launch (start us, length us, event | category | flops | bytes accessed | tf_op | source)
XLA Modules:
  0.0 561.0 jit_solution(4432875654553335063)
XLA Ops:
  6.5 1.3 reduce_sum.36
  7.9 1.4 multiply_reduce_fusion
  9.3 2.3 subtract_multiply_fusion
  11.7 0.7 all-gather.8.cloned.1.call-update
  12.4 0.7 all-gather.12.cloned.1.call-update
  13.3 6.2 %all-gather = f32[4,1,768]{2,1,0:T(1,128)S(1)} all-gather(f32[1,1,768]{2,1,0:T(1,128)S(1)} %reshape.49), channel_id=1, replica_groups=mesh['ens'=2,'row'=4,'col'=4] {'col'}, dimensions={0}, use_global_device_ids=true | all-gather | bytes 15360 | tf_op jit(solution)/shard_map/all_gather | solution.py:32
  19.5 0.9 fusion.1
  20.4 57.6 %all-gather.10.cloned.1.call-done = f32[3072,256]{1,0:T(8,128)} async-done(((f32[768,256]{1,0:T(8,128)}), f32[3072,256]{1,0:T(8,128)}) %all-gather.10.cloned.1.call-update) | async-done | bytes 3145744 | tf_op jit(solution)/shard_map/all_gather | solution.py:41
  78.0 28.7 %all-gather.8.cloned.1.call-done = f32[3072,256]{1,0:T(8,128)} async-done(((f32[768,256]{1,0:T(8,128)}), f32[3072,256]{1,0:T(8,128)}) %all-gather.8.cloned.1.call-update) | async-done | bytes 3145744 | tf_op jit(solution)/shard_map/all_gather | solution.py:31
  106.8 40.0 %fusion = f32[3072,3072]{1,0:T(8,128)} fusion(f32[3072,256]{1,0:T(8,128)} %all-gather.8.cloned.1.call-done, f32[3072,256]{1,0:T(8,128)} %all-gather.10.cloned.1.call-done, f32[3072]{0:T(1024)S(1)} %bitcast.15, f32[8,3072]{1,0:T(8,128)S(1)} %fusion.1), kind=kOutput, calls=%fused_computation.1 | convolution fusion | flops 29019340800 | bytes 44150784 | tf_op jit(solution)/shard_map/dot_general | solution.py:57
  146.8 35.2 %fusion.21 = f32[3072,128]{1,0:T(8,128)} fusion(f32[3072,3072]{1,0:T(8,128)} %fusion, f32[3072,128]{1,0:T(8,128)} %all-gather.12.cloned.1.call-done), kind=kOutput, calls=%fused_computation.39 | convolution fusion | flops 14495514624 | bytes 40894464 | tf_op jit(solution)/shard_map/dot_general | solution.py:70
  182.0 28.3 %reduce-scatter.5.cloned.1.call-done = f32[768,128]{1,0:T(8,128)} async-done(((f32[3072,128]{1,0:T(8,128)}), f32[768,128]{1,0:T(8,128)}) %reduce-scatter.5.cloned.1.call-update) | async-done | bytes 393232 | tf_op jit(solution)/shard_map/reduce_scatter | solution.py:88
  210.4 21.1 %all-gather.14.cloned.1.call-done = f32[3072,128]{1,0:T(8,128)} async-done(((f32[768,128]{1,0:T(8,128)}), f32[3072,128]{1,0:T(8,128)}) %all-gather.14.cloned.1.call-update) | async-done | bytes 1572880 | tf_op jit(solution)/shard_map/all_gather | solution.py:89
  231.5 64.4 %fusion.22 = f32[3072,128]{1,0:T(8,128)} fusion(f32[3072,3072]{1,0:T(8,128)} %fusion, f32[3072,128]{1,0:T(8,128)} %all-gather.14.cloned.1.call-done), kind=kOutput, calls=%fused_computation.40 | convolution fusion | flops 14495514624 | bytes 40894464 | tf_op jit(solution)/shard_map/dot_general | solution.py:78
  296.0 0.6 multiply_reduce_fusion.1
  297.2 34.2 %reduce-scatter.7.cloned.1.call-done = f32[768,128]{1,0:T(8,128)} async-done(((f32[3072,128]{1,0:T(8,128)}), f32[768,128]{1,0:T(8,128)}) %reduce-scatter.7.cloned.1.call-update) | async-done | bytes 393232 | tf_op jit(solution)/shard_map/reduce_scatter | solution.py:90
  331.4 1.8 divide_subtract_fusion
  333.3 36.2 %all-gather.16.cloned.1.call-done = f32[3072,128]{1,0:T(8,128)} async-done(((f32[768,128]{1,0:T(8,128)}), f32[3072,128]{1,0:T(8,128)}) %all-gather.16.cloned.1.call-update) | async-done | bytes 1572880 | tf_op jit(solution)/shard_map/all_gather | solution.py:87
  369.4 34.7 %fusion.23 = f32[3072,128]{1,0:T(8,128)} fusion(f32[3072,3072]{1,0:T(8,128)} %fusion, f32[3072,128]{1,0:T(8,128)} %all-gather.16.cloned.1.call-done), kind=kOutput, calls=%fused_computation.41 | convolution fusion | flops 14495514624 | bytes 40894464 | tf_op jit(solution)/shard_map/dot_general | solution.py:70
  404.2 27.1 %reduce-scatter.9.cloned.1.call-done = f32[768,128]{1,0:T(8,128)} async-done(((f32[3072,128]{1,0:T(8,128)}), f32[768,128]{1,0:T(8,128)}) %reduce-scatter.9.cloned.1.call-update) | async-done | bytes 393232 | tf_op jit(solution)/shard_map/reduce_scatter | solution.py:88
  431.4 21.2 %all-gather.18.cloned.1.call-done = f32[3072,128]{1,0:T(8,128)} async-done(((f32[768,128]{1,0:T(8,128)}), f32[3072,128]{1,0:T(8,128)}) %all-gather.18.cloned.1.call-update) | async-done | bytes 1572880 | tf_op jit(solution)/shard_map/all_gather | solution.py:89
  452.6 64.0 %fusion.24 = f32[3072,128]{1,0:T(8,128)} fusion(f32[3072,3072]{1,0:T(8,128)} %fusion, f32[3072,128]{1,0:T(8,128)} %all-gather.18.cloned.1.call-done), kind=kOutput, calls=%fused_computation.42 | convolution fusion | flops 14495514624 | bytes 40894464 | tf_op jit(solution)/shard_map/dot_general | solution.py:78
  516.7 35.4 %reduce-scatter.11.cloned.1.call-done = f32[768,128]{1,0:T(8,128)} async-done(((f32[3072,128]{1,0:T(8,128)}), f32[768,128]{1,0:T(8,128)}) %reduce-scatter.11.cloned.1.call-update) | async-done | bytes 393232 | tf_op jit(solution)/shard_map/reduce_scatter | solution.py:90
  552.1 1.8 multiply_subtract_fusion
  (32 shorter events, 0.6 us)
Async XLA Ops:
  6.5 6.6 %copy-start.2 = (s32[768]{0:T(1024)S(1)}, s32[768]{0:T(1024)}, u32[]{:S(2)}) copy-start(s32[768]{0:T(1024)} %param.7) | copy-start | bytes 9220
  6.5 6.7 %copy-start.3 = (f32[16]{0:T(128)S(1)}, f32[16]{0:T(128)}, u32[]{:S(2)}) copy-start(f32[16]{0:T(128)} %param.8) | copy-start | bytes 196
  6.5 71.5 %all-gather.10.cloned.1.call-start = ((), (), s32[]{:S(2)}) async-start(), calls=%async_computation.5 | async-start | bytes 3932160 | tf_op jit(solution)/shard_map/all_gather | solution.py:41
  11.6 95.1 %all-gather.8.cloned.1.call-start = ((), (), s32[]{:S(2)}) async-start(), calls=%async_computation.4 | async-start | bytes 3932160 | tf_op jit(solution)/shard_map/all_gather | solution.py:31
  12.4 134.4 %all-gather.12.cloned.1.call-start = ((), (), s32[]{:S(2)}) async-start(), calls=%async_computation.6 | async-start | bytes 1966080 | tf_op jit(solution)/shard_map/all_gather | solution.py:87
  13.1 197.2 %reduce-scatter.5.cloned.1.call-start = ((), (), s32[]{:S(2)}) async-start(), calls=%async_computation.7 | async-start | bytes 1966080 | tf_op jit(solution)/shard_map/reduce_scatter | solution.py:88
  182.0 49.5 %all-gather.14.cloned.1.call-start = ((), (), s32[]{:S(2)}) async-start(), calls=%async_computation.8 | async-start | bytes 1966080 | tf_op jit(solution)/shard_map/all_gather | solution.py:89
  210.3 121.1 %copy-start = (f32[768,128]{1,0:T(8,128)S(1)}, f32[768,128]{1,0:T(8,128)}, u32[]{:S(2)}) copy-start(f32[768,128]{1,0:T(8,128)} %param.6) | copy-start | bytes 1179652
  210.3 121.0 %reduce-scatter.7.cloned.1.call-start = ((), (), s32[]{:S(2)}) async-start(), calls=%async_computation.9 | async-start | bytes 1966080 | tf_op jit(solution)/shard_map/reduce_scatter | solution.py:90
  295.9 73.5 %all-gather.16.cloned.1.call-start = ((), (), s32[]{:S(2)}) async-start(), calls=%async_computation.10 | async-start | bytes 1966080 | tf_op jit(solution)/shard_map/all_gather | solution.py:87
  333.2 98.1 %reduce-scatter.9.cloned.1.call-start = ((), (), s32[]{:S(2)}) async-start(), calls=%async_computation.11 | async-start | bytes 1966080 | tf_op jit(solution)/shard_map/reduce_scatter | solution.py:88
  404.2 48.4 %all-gather.18.cloned.1.call-start = ((), (), s32[]{:S(2)}) async-start(), calls=%async_computation.12 | async-start | bytes 1966080 | tf_op jit(solution)/shard_map/all_gather | solution.py:89
  431.4 120.7 %copy-start.1 = (f32[768,128]{1,0:T(8,128)S(1)}, f32[768,128]{1,0:T(8,128)}, u32[]{:S(2)}) copy-start(f32[768,128]{1,0:T(8,128)} %reduce-scatter.7.cloned.1.call-done) | copy-start | bytes 1179652
  431.4 120.7 %reduce-scatter.11.cloned.1.call-start = ((), (), s32[]{:S(2)}) async-start(), calls=%async_computation.13 | async-start | bytes 1966080 | tf_op jit(solution)/shard_map/reduce_scatter | solution.py:90
Sparse Core Ops, SparseCore 0:
  11.8 66.2 all-gather.9
  79.6 27.1 all-gather.7
  108.3 37.0 all-gather.11
  182.1 28.1 reduce-scatter.4
  211.8 19.6 all-gather.13
  296.0 35.2 reduce-scatter.6
  333.3 36.0 all-gather.15
  404.3 27.0 reduce-scatter.8
  432.9 19.6 all-gather.17
  516.8 35.2 reduce-scatter.10
where the time goes:
time: 569 us; the launch traced here: 561 us
  waiting for transfers between devices  291 us (51%)
  matrix products  239 us (42%)
  between operations  14.5 us (3%)
  other arithmetic  9.36 us (2%)
  blocking collectives  6.16 us (1%)
    dot_general x2, matrix products, backward_add(): lax.dot_general(affinity, shard_piece, (((0,), (0,)), ((), ())), precisio...  128 us
    dot_general x2, matrix products, forward_add(): jnp.dot(affinity, shard_piece, precision=lax.Precision.HIGHEST, preferred...  69.9 us
    reduce_scatter x2, waiting for transfers between devices, normal_apply(): lax.psum_scatter(returned, 'row', scatter_dimension=0, tiled=True)  69.6 us
    all_gather x1, waiting for transfers between devices, local(): shard_piece = lax.all_gather(z_own, 'row', axis=0, tiled=True)  57.6 us
    reduce_scatter x2, waiting for transfers between devices, normal_apply(): product = lax.psum_scatter(product, 'col', scatter_dimension=0, tiled=True)  55.4 us
    all_gather x2, waiting for transfers between devices, normal_apply(): returned = backward_add(lax.all_gather(product, 'col', axis=0, tiled=True))  42.3 us
    dot_general x1, matrix products, local(): lax.dot_general(z_rows, shard_piece, (((1,), (1,)), ((), ())), precision=...  40 us
    all_gather x2, waiting for transfers between devices, normal_apply(): product = forward_add(lax.all_gather(field_in, 'row', axis=0, tiled=True))  36.2 us
  transfers between devices with their start and end apart: 10, of which 9 were waited for; matrix products, arithmetic and copies ran while one was open for 7% of the time, Pallas kernels for 0%

commit v1 on v0

v1 whole, which is shorter than its diff:
```python
import jax
import jax.numpy as jnp
from jax import lax
from jax.sharding import PartitionSpec as P


sharpness = 12.0


def standardize(series):
    centered = series - jnp.mean(series, axis=1, keepdims=True)
    spread = jnp.mean(centered * centered, axis=1, keepdims=True)
    return centered * lax.rsqrt(spread + 1e-05)


def split(x):
    high = lax.reduce_precision(x, 8, 7)
    return high.astype(jnp.bfloat16), (x - high).astype(jnp.bfloat16)


def local(series, vectors, damp_class, damp_levels, removed_blocks):
    n_row, n_col = lax.axis_size("row"), lax.axis_size("col")
    row_id = lax.axis_index("row")
    col_id = lax.axis_index("col")
    shard_rows, samples = series.shape
    wide = vectors.shape[1]
    classes = damp_levels.shape[0]
    order = shard_rows * n_row * n_col
    z_own = standardize(series)
    onehot = (damp_class[:, None] == jnp.arange(classes, dtype=jnp.int32)[None, :]).astype(
        jnp.float32
    )
    damping = jnp.sum(onehot * damp_levels[None, :], axis=1)
    weight_own = damping * damping
    z_rows = lax.all_gather(z_own, "col", axis=0, tiled=True)
    z_cols = lax.all_gather(z_own, "row", axis=0, tiled=True)
    tile_rows, tile_cols = z_rows.shape[0], z_cols.shape[0]
    blocks = removed_blocks.shape[0]
    block_size = order // blocks
    row_block = (row_id * tile_rows + jnp.arange(tile_rows, dtype=jnp.int32)) // block_size
    position = jnp.arange(tile_cols, dtype=jnp.int32)
    col_index = (position // shard_rows * n_col + col_id) * shard_rows + position % shard_rows
    col_block = col_index // block_size
    keep = (1 - removed_blocks).astype(jnp.bfloat16)
    row_hot = (row_block[:, None] == jnp.arange(blocks)[None, :]).astype(jnp.bfloat16)
    col_hot = (col_block[:, None] == jnp.arange(blocks)[None, :]).astype(jnp.bfloat16)
    keep_rows = jnp.dot(row_hot, keep, preferred_element_type=jnp.float32).astype(jnp.bfloat16)
    rows_high, rows_low = split(z_rows)
    cols_high, cols_low = split(z_cols * (sharpness / samples))
    scores = lax.dot_general(
        jnp.concatenate([rows_high, rows_low, rows_high], axis=1),
        jnp.concatenate([cols_high, cols_high, cols_low], axis=1),
        (((1,), (1,)), ((), ())),
        preferred_element_type=jnp.float32,
    )
    keep_full = lax.dot_general(
        keep_rows, col_hot, (((1,), (1,)), ((), ())), preferred_element_type=jnp.float32
    )
    t_high, t_low = split(jnp.tanh(scores) * keep_full)
    spectral_scale = 0.5 * order * jnp.mean(damp_levels * damp_levels)

    def multiply(dims, field, fine):
        high, low = split(field)
        dims = ((dims, (0,)), ((), ()))
        both = lax.dot_general(
            t_high,
            jnp.concatenate([high, low], axis=1),
            dims,
            preferred_element_type=jnp.float32,
        )
        out = both[:, :wide] + both[:, wide:]
        if fine:
            out = out + lax.dot_general(t_low, high, dims, preferred_element_type=jnp.float32)
        return out

    def normal_apply(field_in, fine):
        product = multiply((1,), lax.all_gather(field_in, "row", axis=0, tiled=True), fine[0])
        product = lax.psum_scatter(product, "col", scatter_dimension=0, tiled=True)
        product = product * weight_own[:, None]
        returned = multiply((0,), lax.all_gather(product, "col", axis=0, tiled=True), fine[1])
        return lax.psum_scatter(returned, "row", scatter_dimension=0, tiled=True) / spectral_scale

    first_term = normal_apply(vectors, (True, False)) - vectors
    return 2.0 * (normal_apply(first_term, (False, True)) - first_term) - vectors


def solution(mesh):
    placed = (
        P(("ens", "row", "col"), None),
        P(("ens", "row", "col"), None),
        P(("ens", "row", "col")),
        P(),
        P("ens", None),
    )
    return jax.shard_map(
        local, mesh=mesh, in_specs=placed, out_specs=P(("ens", "row", "col"), None), check_vma=False
    )
```

time: 569 us -> 480 us (0.84); the launches traced: 561 us -> 479 us
  matrix products: 239 us -> 125 us
  other arithmetic: 9.36 us -> 29.9 us
  waiting for transfers between devices: 291 us -> 310 us
  blocking collectives: 6.16 us -> 0 us
    dot_general x6 -> x8, matrix products: 239 us -> 125 us  [the longest x4 40.2 us: multiply(): lax.dot_general(t_high, jnp.concatenate([high, low], axis=1), dims, prefe...]
    all_gather x6, waiting for transfers between devices: 165 us -> 183 us  [the longest x1 61.2 us: local(): z_cols = lax.all_gather(z_own, 'row', axis=0, tiled=True)]
    convert_element_type x0 -> x6, other arithmetic: none -> 14.1 us  [split(): return (high.astype(jnp.bfloat16), (x - high).astype(jnp.bfloat16))]
    all_gather x1 -> x0, blocking collectives: 6.16 us -> none  [local(): lax.all_gather(damping, 'col', axis=0, tiled=True)]
  transfers between devices with their start and end apart: 10 -> 10, of which waited for: 9 -> 10; matrix products, arithmetic and copies ran while one was open for 7% -> 5% of each run, Pallas kernels for 0% -> 0%
where the time goes in v1:
time: 480 us; the launch traced here: 479 us
  waiting for transfers between devices  310 us (65%)
  matrix products  125 us (26%)
  other arithmetic  29.9 us (6%)
  between operations  14.3 us (3%)
    reduce_scatter x2, waiting for transfers between devices, normal_apply(): lax.psum_scatter(returned, 'row', scatter_dimension=0, tiled=True)  69.6 us
    all_gather x1, waiting for transfers between devices, local(): z_cols = lax.all_gather(z_own, 'row', axis=0, tiled=True)  61.2 us
    all_gather x2, waiting for transfers between devices, normal_apply(): lax.all_gather(field_in, 'row', axis=0, tiled=True)  56.4 us
    reduce_scatter x2, waiting for transfers between devices, normal_apply(): product = lax.psum_scatter(product, 'col', scatter_dimension=0, tiled=True)  55.3 us
    dot_general x4, matrix products, multiply(): lax.dot_general(t_high, jnp.concatenate([high, low], axis=1), dims, prefe...  40.2 us
    all_gather x2, waiting for transfers between devices, normal_apply(): lax.all_gather(product, 'col', axis=0, tiled=True)  39.1 us
    dot_general x1, matrix products, local(): lax.dot_general(jnp.concatenate([rows_high, rows_low, rows_high], axis=1)...  36.5 us
    dot_general x2, matrix products, multiply(): lax.dot_general(t_low, high, dims, preferred_element_type=jnp.float32)  32.8 us
  transfers between devices with their start and end apart: 10, of which 10 were waited for; matrix products, arithmetic and copies ran while one was open for 5% of the time, Pallas kernels for 0%

profile of v1, /device:TPU:0, one launch (start us, length us, event | category | flops | bytes accessed | tf_op | source)
XLA Modules:
  0.0 479.3 jit_solution(17580360636062890352)
XLA Ops:
  10.1 2.3 subtract_multiply_fusion
  13.2 15.3 %fusion.43 = f32[3072,3072]{1,0:T(8,128)} fusion(s32[3072]{0:T(1024)S(1)} %get-tuple-element.19, s32[3072]{0:T(1024)S(1)} %get-tuple-element.20, s32[32,32]{1,0:T(8,128)S(1)} %copy-done.3), kind=kOutput, calls=%fused_computation.57 | convolution fusion | flops 610568192 | bytes 37777408 | tf_op jit(solution)/shard_map/dot_general | solution.py:56
  28.5 20.3 %all-gather.11.cloned.1.call-done = f32[3072,128]{1,0:T(8,128)} async-done(((f32[768,128]{1,0:T(8,128)}), f32[3072,128]{1,0:T(8,128)}) %all-gather.11.cloned.1.call-update) | async-done | bytes 1572880 | tf_op jit(solution)/shard_map/all_gather | solution.py:77
  48.8 2.8 fusion.23
  51.6 61.2 %all-gather.9.cloned.1.call-done = f32[3072,256]{1,0:T(8,128)} async-done(((f32[768,256]{1,0:T(8,128)}), f32[3072,256]{1,0:T(8,128)}) %all-gather.9.cloned.1.call-update) | async-done | bytes 3145744 | tf_op jit(solution)/shard_map/all_gather | solution.py:36
  112.7 2.3 reduce-precision_convert_fusion.1
  115.1 26.4 %all-gather.7.cloned.1.call-done = f32[3072,256]{1,0:T(8,128)} async-done(((f32[768,256]{1,0:T(8,128)}), f32[3072,256]{1,0:T(8,128)}) %all-gather.7.cloned.1.call-update) | async-done | bytes 3145744 | tf_op jit(solution)/shard_map/all_gather | solution.py:35
  141.5 4.0 fusion.21
  145.5 36.5 %reduce-precision_convert_fusion = (bf16[3072,3072]{1,0:T(8,128)(2,1)}, f32[3072,3072]{1,0:T(8,128)}) fusion(f32[3072,3072]{1,0:T(8,128)} %fusion.43, bf16[3072,256]{1,0:T(8,128)(2,1)S(1)} %get-tuple-element.6, bf16[3072,256]{1,0:T(8,128)(2,1)S(1)} %get-tuple-element.5, bf16[3072,256]{1,0:T(8,128)(2,1)} %get-tuple-element.8, ...), kind=kOutput, calls=%fused_computation.1 | convolution fusion | flops 14552137728 | bytes 100663296 | tf_op jit(solution)/shard_map/dot_general | solution.py:50
  182.0 10.7 %fusion.27 = f32[3072,256]{1,0:T(8,128)} fusion(bf16[3072,3072]{1,0:T(8,128)(2,1)} %get-tuple-element.17, bf16[3072,128]{1,0:T(8,128)(2,1)} %get-tuple-element.15, bf16[3072,128]{1,0:T(8,128)(2,1)} %get-tuple-element.16), kind=kOutput, calls=%fused_computation.41 | convolution fusion | flops 4834983936 | bytes 23592960 | tf_op jit(solution)/shard_map/dot_general | solution.py:65
  192.7 16.4 %fusion.18 = f32[3072,128]{1,0:T(8,128)} fusion(bf16[3072,128]{1,0:T(8,128)(2,1)S(1)} %copy-done.1, f32[3072,3072]{1,0:T(8,128)} %get-tuple-element.18, f32[3072,256]{1,0:T(8,128)} %fusion.27), kind=kOutput, calls=%fused_computation.21 | convolution fusion | flops 2445017088 | bytes 43253760 | tf_op jit(solution)/shard_map/dot_general | solution.py:73
  209.3 28.1 %reduce-scatter.5.cloned.1.call-done = f32[768,128]{1,0:T(8,128)} async-done(((f32[3072,128]{1,0:T(8,128)}), f32[768,128]{1,0:T(8,128)}) %reduce-scatter.5.cloned.1.call-update) | async-done | bytes 393232 | tf_op jit(solution)/shard_map/reduce_scatter | solution.py:78
  237.4 1.9 broadcast_multiply_fusion.1
  239.6 19.6 %all-gather.13.cloned.1.call-done = f32[3072,128]{1,0:T(8,128)} async-done(((f32[768,128]{1,0:T(8,128)}), f32[3072,128]{1,0:T(8,128)}) %all-gather.13.cloned.1.call-update) | async-done | bytes 1572880 | tf_op jit(solution)/shard_map/all_gather | solution.py:80
  260.8 9.4 %fusion.31 = f32[3072,256]{1,0:T(8,128)S(1)} fusion(bf16[3072,3072]{1,0:T(8,128)(2,1)} %get-tuple-element.17, bf16[3072,128]{1,0:T(8,128)(2,1)S(1)} %get-tuple-element.14, bf16[3072,128]{1,0:T(8,128)(2,1)S(1)} %get-tuple-element.13), kind=kOutput, calls=%fused_computation.45 | convolution fusion | flops 4834983936 | bytes 23592960 | tf_op jit(solution)/shard_map/dot_general | solution.py:65
  272.8 34.2 %reduce-scatter.7.cloned.1.call-done = f32[768,128]{1,0:T(8,128)} async-done(((f32[3072,128]{1,0:T(8,128)}), f32[768,128]{1,0:T(8,128)}) %reduce-scatter.7.cloned.1.call-update) | async-done | bytes 393232 | tf_op jit(solution)/shard_map/reduce_scatter | solution.py:81
  308.8 36.2 %all-gather.15.cloned.1.call-done = f32[3072,128]{1,0:T(8,128)} async-done(((f32[768,128]{1,0:T(8,128)}), f32[3072,128]{1,0:T(8,128)}) %all-gather.15.cloned.1.call-update) | async-done | bytes 1572880 | tf_op jit(solution)/shard_map/all_gather | solution.py:77
  346.6 9.2 %fusion.35 = f32[3072,256]{1,0:T(8,128)S(1)} fusion(bf16[3072,3072]{1,0:T(8,128)(2,1)} %get-tuple-element.17, bf16[3072,128]{1,0:T(8,128)(2,1)S(1)} %get-tuple-element.12, bf16[3072,128]{1,0:T(8,128)(2,1)S(1)} %get-tuple-element.11), kind=kOutput, calls=%fused_computation.49 | convolution fusion | flops 4834983936 | bytes 23592960 | tf_op jit(solution)/shard_map/dot_general | solution.py:65
  357.2 27.1 %reduce-scatter.9.cloned.1.call-done = f32[768,128]{1,0:T(8,128)} async-done(((f32[3072,128]{1,0:T(8,128)}), f32[768,128]{1,0:T(8,128)}) %reduce-scatter.9.cloned.1.call-update) | async-done | bytes 393232 | tf_op jit(solution)/shard_map/reduce_scatter | solution.py:78
  384.4 1.9 broadcast_multiply_fusion
  386.6 19.5 %all-gather.17.cloned.1.call-done = f32[3072,128]{1,0:T(8,128)} async-done(((f32[768,128]{1,0:T(8,128)}), f32[3072,128]{1,0:T(8,128)}) %all-gather.17.cloned.1.call-update) | async-done | bytes 1572880 | tf_op jit(solution)/shard_map/all_gather | solution.py:80
  407.8 11.0 %fusion.39 = f32[3072,256]{1,0:T(8,128)} fusion(bf16[3072,3072]{1,0:T(8,128)(2,1)} %get-tuple-element.17, bf16[3072,128]{1,0:T(8,128)(2,1)S(1)} %get-tuple-element.9, bf16[3072,128]{1,0:T(8,128)(2,1)S(1)} %get-tuple-element.10), kind=kOutput, calls=%fused_computation.53 | convolution fusion | flops 4834983936 | bytes 23592960 | tf_op jit(solution)/shard_map/dot_general | solution.py:65
  418.7 16.4 %fusion.15 = f32[3072,128]{1,0:T(8,128)} fusion(bf16[3072,128]{1,0:T(8,128)(2,1)S(1)} %get-tuple-element.10, f32[3072,3072]{1,0:T(8,128)} %get-tuple-element.18, f32[3072,256]{1,0:T(8,128)} %fusion.39), kind=kOutput, calls=%fused_computation.20 | convolution fusion | flops 2445017088 | bytes 43253760 | tf_op jit(solution)/shard_map/dot_general | solution.py:73
  435.2 35.4 %reduce-scatter.11.cloned.1.call-done = f32[768,128]{1,0:T(8,128)} async-done(((f32[3072,128]{1,0:T(8,128)}), f32[768,128]{1,0:T(8,128)}) %reduce-scatter.11.cloned.1.call-update) | async-done | bytes 393232 | tf_op jit(solution)/shard_map/reduce_scatter | solution.py:81
  (47 shorter events, 16.9 us)
Async XLA Ops:
  6.5 6.7 %copy-start.3 = (s32[32,32]{1,0:T(8,128)S(1)}, s32[32,32]{1,0:T(8,128)}, u32[]{:S(2)}) copy-start(s32[32,32]{1,0:T(8,128)} %param.9) | copy-start | bytes 12292
  6.5 42.2 %all-gather.11.cloned.1.call-start = ((), (), s32[]{:S(2)}) async-start(), calls=%async_computation.6 | async-start | bytes 1966080 | tf_op jit(solution)/shard_map/all_gather | solution.py:77
  7.3 105.5 %all-gather.9.cloned.1.call-start = ((), (), s32[]{:S(2)}) async-start(), calls=%async_computation.5 | async-start | bytes 3932160 | tf_op jit(solution)/shard_map/all_gather | solution.py:36
  12.4 129.1 %all-gather.7.cloned.1.call-start = ((), (), s32[]{:S(2)}) async-start(), calls=%async_computation.4 | async-start | bytes 3932160 | tf_op jit(solution)/shard_map/all_gather | solution.py:35
  13.1 224.3 %reduce-scatter.5.cloned.1.call-start = ((), (), s32[]{:S(2)}) async-start(), calls=%async_computation.7 | async-start | bytes 1966080 | tf_op jit(solution)/shard_map/reduce_scatter | solution.py:78
  182.0 10.7 %copy-start.1 = (bf16[3072,128]{1,0:T(8,128)(2,1)S(1)}, bf16[3072,128]{1,0:T(8,128)(2,1)}, u32[]{:S(2)}) copy-start(bf16[3072,128]{1,0:T(8,128)(2,1)} %get-tuple-element.16) | copy-start | bytes 2359300
  192.7 16.5 %copy-start.4 = (s32[768]{0:T(1024)S(1)}, s32[768]{0:T(1024)}, u32[]{:S(2)}) copy-start(s32[768]{0:T(1024)} %param.7) | copy-start | bytes 9220
  192.7 16.5 %copy-start.5 = (f32[16]{0:T(128)S(1)}, f32[16]{0:T(128)}, u32[]{:S(2)}) copy-start(f32[16]{0:T(128)} %param.8) | copy-start | bytes 196
  209.1 50.1 %all-gather.13.cloned.1.call-start = ((), (), s32[]{:S(2)}) async-start(), calls=%async_computation.8 | async-start | bytes 1966080 | tf_op jit(solution)/shard_map/all_gather | solution.py:80
  239.3 67.6 %reduce-scatter.7.cloned.1.call-start = ((), (), s32[]{:S(2)}) async-start(), calls=%async_computation.9 | async-start | bytes 1966080 | tf_op jit(solution)/shard_map/reduce_scatter | solution.py:81
  270.2 36.8 %copy-start = (f32[768,128]{1,0:T(8,128)S(1)}, f32[768,128]{1,0:T(8,128)}, u32[]{:S(2)}) copy-start(f32[768,128]{1,0:T(8,128)} %param.6) | copy-start | bytes 1179652
  271.5 73.5 %all-gather.15.cloned.1.call-start = ((), (), s32[]{:S(2)}) async-start(), calls=%async_computation.10 | async-start | bytes 1966080 | tf_op jit(solution)/shard_map/all_gather | solution.py:77
  308.8 75.6 %reduce-scatter.9.cloned.1.call-start = ((), (), s32[]{:S(2)}) async-start(), calls=%async_computation.11 | async-start | bytes 1966080 | tf_op jit(solution)/shard_map/reduce_scatter | solution.py:78
  357.2 48.9 %all-gather.17.cloned.1.call-start = ((), (), s32[]{:S(2)}) async-start(), calls=%async_computation.12 | async-start | bytes 1966080 | tf_op jit(solution)/shard_map/all_gather | solution.py:80
  386.3 84.3 %reduce-scatter.11.cloned.1.call-start = ((), (), s32[]{:S(2)}) async-start(), calls=%async_computation.13 | async-start | bytes 1966080 | tf_op jit(solution)/shard_map/reduce_scatter | solution.py:81
  418.7 51.9 %copy-start.2 = (f32[768,128]{1,0:T(8,128)S(1)}, f32[768,128]{1,0:T(8,128)}, u32[]{:S(2)}) copy-start(f32[768,128]{1,0:T(8,128)} %reduce-scatter.7.cloned.1.call-done) | copy-start | bytes 1179652
Sparse Core Ops, SparseCore 0:
  8.9 39.7 all-gather.10
  50.3 62.3 all-gather.8
  114.3 27.1 all-gather.6
  209.2 28.1 reduce-scatter.4
  239.5 19.6 all-gather.12
  271.6 35.2 reduce-scatter.6
  308.9 36.0 all-gather.14
  357.3 27.0 reduce-scatter.8
  386.4 19.6 all-gather.16
  435.3 35.2 reduce-scatter.10

commit v2 on v1

--- a/solution.py
+++ b/solution.py
@@ -1,6 +1,10 @@
+import functools
+
 import jax
 import jax.numpy as jnp
 from jax import lax
+from jax.experimental import pallas as pl
+from jax.experimental.pallas import tpu as pltpu
 from jax.sharding import PartitionSpec as P
 
 
@@ -16,6 +20,323 @@
 def split(x):
     high = lax.reduce_precision(x, 8, 7)
     return high.astype(jnp.bfloat16), (x - high).astype(jnp.bfloat16)
+
+
+MESH = pl.DeviceIdType.MESH
+
+
+def send(src, dst, send_sem, recv_sem, device):
+    return pltpu.make_async_remote_copy(
+        src_ref=src,
+        dst_ref=dst,
+        send_sem=send_sem,
+        recv_sem=recv_sem,
+        device_id=device,
+        device_id_type=MESH,
+    )
+
+
+def greet_line(n, me):
+    barrier = pltpu.get_barrier_semaphore()
+
+    @pl.when(me > 0)
+    def _():
+        pl.semaphore_signal(barrier, inc=1, device_id={"row": me - 1}, device_id_type=MESH)
+
+    @pl.when(me < n - 1)
+    def _():
+        pl.semaphore_signal(barrier, inc=1, device_id={"row": me + 1}, device_id_type=MESH)
+
+    inside = (me > 0) & (me < n - 1)
+
+    @pl.when(inside)
+    def _():
+        pl.semaphore_wait(barrier, 2)
+
+    @pl.when(jnp.logical_not(inside))
+    def _():
+        pl.semaphore_wait(barrier, 1)
+
+
+def line_gather_kernel(n, own_ref, out_ref, send_right, recv_right, send_left, recv_left):
+    me = lax.axis_index("row")
+    greet_line(n, me)
+    out_ref[me] = own_ref[...]
+
+    def right(block, step, device):
+        place = out_ref.at[block]
+        return send(place, place, send_right.at[step], recv_right.at[step], {"row": device})
+
+    def left(block, step, device):
+        place = out_ref.at[block]
+        return send(place, place, send_left.at[step], recv_left.at[step], {"row": device})
+
+    for step in range(n - 1):
+
+        @pl.when((me - step >= 0) & (me < n - 1))
+        def _():
+            right(me - step, step, me + 1).start()
+
+        @pl.when((me + step < n) & (me > 0))
+        def _():
+            left(me + step, step, me - 1).start()
+
+        @pl.when(me - 1 - step >= 0)
+        def _():
+            right(me - 1 - step, step, me - 1).wait_recv()
+
+        @pl.when(me + 1 + step < n)
+        def _():
+            left(me + 1 + step, step, me + 1).wait_recv()
+
+    for step in range(n - 1):
+
+        @pl.when((me - step >= 0) & (me < n - 1))
+        def _():
+            right(me - step, step, me + 1).wait_send()
+
+        @pl.when((me + step < n) & (me > 0))
+        def _():
+            left(me + step, step, me - 1).wait_send()
+
+
+def line_gather(own, n, collective_id):
+    rows, wide = own.shape
+    return pl.pallas_call(
+        functools.partial(line_gather_kernel, n),
+        out_shape=jax.ShapeDtypeStruct((n, rows, wide), own.dtype),
+        in_specs=[pl.BlockSpec(memory_space=pltpu.VMEM)],
+        out_specs=pl.BlockSpec(memory_space=pltpu.VMEM),
+        scratch_shapes=[pltpu.SemaphoreType.DMA((n - 1,))] * 4,
+        compiler_params=pltpu.CompilerParams(
+            collective_id=collective_id, has_side_effects=True, vmem_limit_bytes=32 * 2**20
+        ),
+    )(own).reshape(n * rows, wide)
+
+
+def line_scatter_kernel(
+    n, parts_ref, out_ref, from_left, from_right, send_right, recv_right, send_left, recv_left
+):
+    me = lax.axis_index("row")
+    mirror = n - 1 - me
+    greet_line(n, me)
+
+    def target(step, place):
+        return n - 1 - (step - place)
+
+    def right(src, step, block, device):
+        return send(
+            src, from_left.at[block], send_right.at[step], recv_right.at[step], {"row": device}
+        )
+
+    def left(src, step, block, device):
+        return send(
+            src, from_right.at[block], send_left.at[step], recv_left.at[step], {"row": device}
+        )
+
+    for step in range(n - 1):
+        block_right = target(step, me)
+        block_left = n - 1 - target(step, mirror)
+        sends_right = (step >= me) & (me < n - 1)
+        sends_left = (step >= mirror) & (mirror < n - 1)
+
+        @pl.when(sends_right & (me == 0))
+        def _():
+            right(parts_ref.at[block_right], step, block_right, me + 1).start()
+
+        @pl.when(sends_right & (me > 0))
+        def _():
+            right(from_left.at[block_right], step, block_right, me + 1).start()
+
+        @pl.when(sends_left & (mirror == 0))
+        def _():
+            left(parts_ref.at[block_left], step, block_left, me - 1).start()
+
+        @pl.when(sends_left & (mirror > 0))
+        def _():
+            left(from_right.at[block_left], step, block_left, me - 1).start()
+
+        coming_right = target(step, me - 1)
+        coming_left = n - 1 - target(step, mirror - 1)
+
+        @pl.when((me >= 1) & (step >= me - 1))
+        def _():
+            right(from_left.at[coming_right], step, coming_right, me - 1).wait_recv()
+
+            @pl.when(coming_right > me)
+            def _():
+                from_left[coming_right] = from_left[coming_right] + parts_ref[coming_right]
+
+        @pl.when((mirror >= 1) & (step >= mirror - 1))
+        def _():
+            left(from_right.at[coming_left], step, coming_left, me + 1).wait_recv()
+
+            @pl.when(coming_left < me)
+            def _():
+                from_right[coming_left] = from_right[coming_left] + parts_ref[coming_left]
+
+    out_ref[...] = parts_ref[me]
+
+    @pl.when(me > 0)
+    def _():
+        out_ref[...] = out_ref[...] + from_left[me]
+
+    @pl.when(mirror > 0)
+    def _():
+        out_ref[...] = out_ref[...] + from_right[me]
+
+    for step in range(n - 1):
+        block_right = target(step, me)
+        block_left = n - 1 - target(step, mirror)
+
+        @pl.when((step >= me) & (me < n - 1))
+        def _():
+            right(from_left.at[block_right], step, block_right, me + 1).wait_send()
+
+        @pl.when((step >= mirror) & (mirror < n - 1))
+        def _():
+            left(from_right.at[block_left], step, block_left, me - 1).wait_send()
+
+
+def line_scatter(partial, n, collective_id):
+    rows, wide = partial.shape[0] // n, partial.shape[1]
+    return pl.pallas_call(
+        functools.partial(line_scatter_kernel, n),
+        out_shape=jax.ShapeDtypeStruct((rows, wide), partial.dtype),
+        in_specs=[pl.BlockSpec(memory_space=pltpu.VMEM)],
+        out_specs=pl.BlockSpec(memory_space=pltpu.VMEM),
+        scratch_shapes=[pltpu.VMEM((n, rows, wide), partial.dtype)] * 2
+        + [pltpu.SemaphoreType.DMA((n - 1,))] * 4,
+        compiler_params=pltpu.CompilerParams(
+            collective_id=collective_id, has_side_effects=True, vmem_limit_bytes=32 * 2**20
+        ),
+    )(partial.reshape(n, rows, wide))
+
+
+def greet_plane(nx, col):
+    core, x = col % 2, col // 2
+    partner = x * 2 + 1 - core
+    peers = [lax.rem(x + step, nx) * 2 + core for step in range(1, nx)]
+    barrier = pltpu.get_barrier_semaphore()
+    for device in [partner] + peers:
+        pl.semaphore_signal(barrier, inc=1, device_id={"col": device}, device_id_type=MESH)
+    pl.semaphore_wait(barrier, nx)
+    return core, x, partner
+
+
+def spread_plane(nx, core, x, partner, out_ref, send_peer, recv_peer, send_core, recv_core):
+    copies = []
+    own = out_ref.at[x, core]
+    for step in range(1, nx):
+        peer = lax.rem(x + step, nx) * 2 + core
+        copies.append(
+            send(own, own, send_peer.at[step - 1], recv_peer.at[step - 1], {"col": peer})
+        )
+        copies[-1].start()
+    copies.append(send(own, own, send_core.at[0], recv_core.at[0], {"col": partner}))
+    copies[-1].start()
+    for step in range(1, nx):
+        origin = lax.rem(x + nx - step, nx)
+        place = out_ref.at[origin, core]
+        send(
+            place, place, send_peer.at[step - 1], recv_peer.at[step - 1], {"col": origin * 2 + core}
+        ).wait_recv()
+        copies.append(send(place, place, send_core.at[step], recv_core.at[step], {"col": partner}))
+        copies[-1].start()
+    for step in range(nx):
+        place = out_ref.at[lax.rem(x + nx - step, nx), 1 - core]
+        send(
+            place, place, send_core.at[step], recv_core.at[step], {"col": partner}
+        ).wait_recv()
+    for copy in copies:
+        copy.wait_send()
+
+
+def plane_gather_kernel(nx, own_ref, out_ref, *sems):
+    core, x, partner = greet_plane(nx, lax.axis_index("col"))
+    out_ref[x, core] = own_ref[...]
+    spread_plane(nx, core, x, partner, out_ref, *sems)
+
+
+def plane_sems(nx):
+    return [pltpu.SemaphoreType.DMA((max(nx - 1, 1),))] * 2 + [pltpu.SemaphoreType.DMA((nx,))] * 2
+
+
+def plane_gather(own, n, collective_id):
+    nx = n // 2
+    rows, wide = own.shape
+    return pl.pallas_call(
+        functools.partial(plane_gather_kernel, nx),
+        out_shape=jax.ShapeDtypeStruct((nx, 2, rows, wide), own.dtype),
+        in_specs=[pl.BlockSpec(memory_space=pltpu.VMEM)],
+        out_specs=pl.BlockSpec(memory_space=pltpu.VMEM),
+        scratch_shapes=plane_sems(nx),
+        compiler_params=pltpu.CompilerParams(
+            collective_id=collective_id, has_side_effects=True, vmem_limit_bytes=32 * 2**20
+        ),
+    )(own).reshape(n * rows, wide)
+
+
+def plane_sum_kernel(
+    nx, parts_ref, weight_ref, out_ref, half, landed, s_half, r_half, s_land, r_land, *sems
+):
+    core, x, partner = greet_plane(nx, lax.axis_index("col"))
+    copies = []
+    order = [lax.rem(x + step, nx) for step in list(range(1, nx)) + [0]]
+    for step, k in enumerate(order):
+        copies.append(
+            send(
+                parts_ref.at[k, 1 - core],
+                half.at[k],
+                s_half.at[step],
+                r_half.at[step],
+                {"col": partner},
+            )
+        )
+        copies[-1].start()
+    for step, k in enumerate(order):
+        copies[step].wait_recv()
+        half[k] = half[k] + parts_ref[k, core]
+        if step < nx - 1:
+            copies.append(
+                send(
+                    half.at[k],
+                    landed.at[step],
+                    s_land.at[step],
+                    r_land.at[step],
+                    {"col": k * 2 + core},
+                )
+            )
+            copies[-1].start()
+    total = half[x]
+    for step in range(nx - 1):
+        copies[nx + step].wait_recv()
+        total = total + landed[step]
+    out_ref[x, core] = total * weight_ref[...]
+    spread_plane(nx, core, x, partner, out_ref, *sems)
+    for copy in copies:
+        copy.wait_send()
+
+
+def plane_sum(partial, weight, n, collective_id):
+    nx = n // 2
+    rows, wide = partial.shape[0] // n, partial.shape[1]
+    return pl.pallas_call(
+        functools.partial(plane_sum_kernel, nx),
+        out_shape=jax.ShapeDtypeStruct((nx, 2, rows, wide), partial.dtype),
+        in_specs=[pl.BlockSpec(memory_space=pltpu.VMEM)] * 2,
+        out_specs=pl.BlockSpec(memory_space=pltpu.VMEM),
+        scratch_shapes=[
+            pltpu.VMEM((nx, rows, wide), partial.dtype),
+            pltpu.VMEM((max(nx - 1, 1), rows, wide), partial.dtype),
+        ]
+        + [pltpu.SemaphoreType.DMA((nx,))] * 2
+        + [pltpu.SemaphoreType.DMA((max(nx - 1, 1),))] * 2
+        + plane_sems(nx),
+        compiler_params=pltpu.CompilerParams(
+            collective_id=collective_id, has_side_effects=True, vmem_limit_bytes=32 * 2**20
+        ),
+    )(partial.reshape(nx, 2, rows, wide), weight).reshape(n * rows, wide)
 
 
 def local(series, vectors, damp_class, damp_levels, removed_blocks):
@@ -33,7 +354,7 @@
     damping = jnp.sum(onehot * damp_levels[None, :], axis=1)
     weight_own = damping * damping
     z_rows = lax.all_gather(z_own, "col", axis=0, tiled=True)
-    z_cols = lax.all_gather(z_own, "row", axis=0, tiled=True)
+    z_cols = line_gather(z_own, n_row, 0)
     tile_rows, tile_cols = z_rows.shape[0], z_cols.shape[0]
     blocks = removed_blocks.shape[0]
     block_size = order // blocks
@@ -73,15 +394,18 @@
             out = out + lax.dot_general(t_low, high, dims, preferred_element_type=jnp.float32)
         return out
 
-    def normal_apply(field_in, fine):
-        product = multiply((1,), lax.all_gather(field_in, "row", axis=0, tiled=True), fine[0])
-        product = lax.psum_scatter(product, "col", scatter_dimension=0, tiled=True)
-        product = product * weight_own[:, None]
-        returned = multiply((0,), lax.all_gather(product, "col", axis=0, tiled=True), fine[1])
-        return lax.psum_scatter(returned, "row", scatter_dimension=0, tiled=True) / spectral_scale
-
-    first_term = normal_apply(vectors, (True, False)) - vectors
-    return 2.0 * (normal_apply(first_term, (False, True)) - first_term) - vectors
+    weight_wide = jnp.broadcast_to(weight_own[:, None], (shard_rows, wide))
+
+    def normal_apply(field_cols, fine):
+        product = multiply((1,), field_cols, fine[0])
+        product = plane_sum(product, weight_wide, n_col, 2)
+        returned = multiply((0,), product, fine[1])
+        return line_scatter(returned, n_row, 3) / spectral_scale
+
+    vectors_cols = lax.all_gather(vectors, "row", axis=0, tiled=True)
+    first_term = normal_apply(vectors_cols, (True, False)) - vectors
+    first_cols = line_gather(first_term, n_row, 1)
+    return 2.0 * (normal_apply(first_cols, (False, True)) - first_term) - vectors
 
 
 def solution(mesh):

time: 480 us -> 365 us (0.76)
  waiting for transfers between devices: 310 us -> 0.73 us
  Pallas kernels: 0 us -> 217 us
  other arithmetic: 29.9 us -> 15.3 us
  matrix products: 125 us -> 116 us
    pallas_call x0 -> x6, Pallas kernels: none -> 217 us  [the longest x2 107 us: line_gather(): pl.pallas_call(functools.partial(line_gather_kernel, n), out_shape=jax.Sh...]
    all_gather x5 -> x1, waiting for transfers between devices: 157 us -> 0.01 us  [local(): vectors_cols = lax.all_gather(vectors, 'row', axis=0, tiled=True)]
    reduce_scatter x4 -> x0, waiting for transfers between devices: 125 us -> none  [the longest x2 69.6 us: normal_apply(): lax.psum_scatter(returned, 'row', scatter_dimension=0, tiled=True)]
    all_gather x1, waiting for transfers between devices: 26.4 us -> 0.01 us  [local(): z_rows = lax.all_gather(z_own, 'col', axis=0, tiled=True)]
    dot_general x4, matrix products: 40.2 us -> 33.8 us  [multiply(): lax.dot_general(t_high, jnp.concatenate([high, low], axis=1), dims, prefe...]
    convert_element_type x6, other arithmetic: 14.1 us -> 8.11 us  [split(): return (high.astype(jnp.bfloat16), (x - high).astype(jnp.bfloat16))]
  transfers between devices with their start and end apart: 10 -> 2, of which waited for: 10 -> 0; matrix products, arithmetic and copies ran while one was open for 5% -> 7% of each run, Pallas kernels for 0% -> 22%
where the time goes in v2:
time: 365 us
  Pallas kernels  217 us (59%)
  matrix products  116 us (32%)
  other arithmetic  15.3 us (4%)
  between operations  14.4 us (4%)
    pallas_call x2, Pallas kernels, line_gather(): pl.pallas_call(functools.partial(line_gather_kernel, n), out_shape=jax.Sh...  107 us
    pallas_call x2, Pallas kernels, line_scatter(): pl.pallas_call(functools.partial(line_scatter_kernel, n), out_shape=jax.S...  60.8 us
    pallas_call x2, Pallas kernels, plane_sum(): pl.pallas_call(functools.partial(plane_sum_kernel, nx), out_shape=jax.Sha...  48.9 us
    dot_general x1, matrix products, local(): lax.dot_general(jnp.concatenate([rows_high, rows_low, rows_high], axis=1)...  36.3 us
    dot_general x4, matrix products, multiply(): lax.dot_general(t_high, jnp.concatenate([high, low], axis=1), dims, prefe...  33.8 us
    dot_general x2, matrix products, multiply(): lax.dot_general(t_low, high, dims, preferred_element_type=jnp.float32)  30.6 us
    dot_general x1, matrix products, local(): lax.dot_general(keep_rows, col_hot, (((1,), (1,)), ((), ())), preferred_e...  15 us
    convert_element_type x6, other arithmetic, split(): return (high.astype(jnp.bfloat16), (x - high).astype(jnp.bfloat16))  8.11 us
  transfers between devices with their start and end apart: 2, of which 0 were waited for; matrix products, arithmetic and copies ran while one was open for 7% of the time, Pallas kernels for 22%

profile of v2, /device:TPU:0, one launch (start us, length us, event | category | flops | bytes accessed | tf_op | source)
XLA Modules:
  0.0 364.5 jit_solution(4532557508451294826)
XLA Ops:
  6.5 0.7 all-gather.5.cloned.1.call-update
  7.3 1.3 reduce_sum.36
  8.6 1.4 multiply_reduce_fusion
  10.1 2.3 subtract_multiply_fusion.own_ref
  12.5 1.1 copy-done
  13.6 81.0 %shard_map.55 = f32[4,768,256]{2,1,0:T(8,128)S(1)} custom-call(f32[768,256]{1,0:T(8,128)S(1)} %copy-done), custom_call_target="tpu_custom_call" | custom-call | tf_op jit(solution)/shard_map/pallas_call | solution.py:105
  94.7 0.6 multiply_reduce_fusion.1
  96.3 0.5 reduce-precision_convert_fusion.1
  97.0 15.0 %fusion.43 = f32[3072,3072]{1,0:T(8,128)} fusion(s32[3072]{0:T(1024)S(1)} %get-tuple-element.19, s32[3072]{0:T(1024)S(1)} %get-tuple-element.20, s32[32,32]{1,0:T(8,128)S(1)} %copy-done.3), kind=kOutput, calls=%fused_computation.58 | convolution fusion | flops 610568192 | bytes 37777408 | tf_op jit(solution)/shard_map/dot_general | solution.py:377
  111.9 2.8 fusion.23
  114.8 4.0 %fusion.21 = (bf16[3072,256]{1,0:T(8,128)(2,1)}, bf16[3072,256]{1,0:T(8,128)(2,1)}) fusion(f32[3072,256]{1,0:T(8,128)} %all-gather.3.cloned.1.call-done), kind=kLoop, calls=%fused_computation.23 | loop fusion | flops 3145728 | bytes 6291456 | tf_op jit(solution)/shard_map/convert_element_type | solution.py:22
  118.8 36.3 %reduce-precision_convert_fusion = (bf16[3072,3072]{1,0:T(8,128)(2,1)}, f32[3072,3072]{1,0:T(8,128)}) fusion(f32[3072,3072]{1,0:T(8,128)} %fusion.43, bf16[3072,256]{1,0:T(8,128)(2,1)S(1)} %get-tuple-element.6, bf16[3072,256]{1,0:T(8,128)(2,1)S(1)} %get-tuple-element.5, bf16[3072,256]{1,0:T(8,128)(2,1)} %get-tuple-element.8, ...), kind=kOutput, calls=%fused_computation.1 | convolution fusion | flops 14552137728 | bytes 100663296 | tf_op jit(solution)/shard_map/dot_general | solution.py:371
  155.1 10.7 %fusion.27 = f32[3072,256]{1,0:T(8,128)} fusion(bf16[3072,3072]{1,0:T(8,128)(2,1)} %get-tuple-element.17, bf16[3072,128]{1,0:T(8,128)(2,1)} %get-tuple-element.15, bf16[3072,128]{1,0:T(8,128)(2,1)} %get-tuple-element.16), kind=kOutput, calls=%fused_computation.41 | convolution fusion | flops 4834983936 | bytes 23592960 | tf_op jit(solution)/shard_map/dot_general | solution.py:386
  165.7 15.3 %fusion.18 = f32[3072,128]{1,0:T(8,128)S(1)} fusion(bf16[3072,128]{1,0:T(8,128)(2,1)S(1)} %copy-done.2, f32[3072,3072]{1,0:T(8,128)} %get-tuple-element.18, f32[3072,256]{1,0:T(8,128)} %fusion.27), kind=kOutput, calls=%fused_computation.21 | convolution fusion | flops 2445017088 | bytes 43253760 | tf_op jit(solution)/shard_map/dot_general | solution.py:394
  181.2 24.4 %shard_map.56 = f32[2,2,768,128]{3,2,1,0:T(8,128)S(1)} custom-call(f32[2,2,768,128]{3,2,1,0:T(8,128)S(1)} %bitcast.22, f32[768,128]{1,0:T(8,128)S(1)} %broadcast_in_dim.2.weight_ref), custom_call_target="tpu_custom_call" | custom-call | tf_op jit(solution)/shard_map/pallas_call | solution.py:324
  205.9 9.7 %fusion.31 = f32[3072,256]{1,0:T(8,128)S(1)} fusion(bf16[3072,3072]{1,0:T(8,128)(2,1)} %get-tuple-element.17, bf16[3072,128]{1,0:T(8,128)(2,1)S(1)} %get-tuple-element.14, bf16[3072,128]{1,0:T(8,128)(2,1)S(1)} %get-tuple-element.13), kind=kOutput, calls=%fused_computation.45 | convolution fusion | flops 4834983936 | bytes 23592960 | tf_op jit(solution)/shard_map/dot_general | solution.py:386
  215.8 30.9 %shard_map.57 = f32[768,128]{1,0:T(8,128)S(1)} custom-call(f32[4,768,128]{2,1,0:T(8,128)S(1)} %bitcast.25), custom_call_target="tpu_custom_call" | custom-call | tf_op jit(solution)/shard_map/pallas_call | solution.py:203
  246.7 26.3 %shard_map.58 = f32[4,768,128]{2,1,0:T(8,128)S(1)} custom-call(f32[768,128]{1,0:T(8,128)S(1)} %divide_subtract_fusion.own_ref), custom_call_target="tpu_custom_call" | custom-call | tf_op jit(solution)/shard_map/pallas_call | solution.py:105
  273.4 5.7 %fusion.35 = f32[3072,256]{1,0:T(8,128)S(1)} fusion(bf16[3072,3072]{1,0:T(8,128)(2,1)S(1)} %bitcast.27, bf16[3072,128]{1,0:T(8,128)(2,1)S(1)} %get-tuple-element.12, bf16[3072,128]{1,0:T(8,128)(2,1)S(1)} %get-tuple-element.11), kind=kOutput, calls=%fused_computation.49 | convolution fusion | flops 4834983936 | bytes 23592960 | tf_op jit(solution)/shard_map/dot_general | solution.py:386
  279.2 24.4 %shard_map.59 = f32[2,2,768,128]{3,2,1,0:T(8,128)S(1)} custom-call(f32[2,2,768,128]{3,2,1,0:T(8,128)S(1)} %bitcast.24, f32[768,128]{1,0:T(8,128)S(1)} %broadcast_in_dim.2.weight_ref), custom_call_target="tpu_custom_call" | custom-call | tf_op jit(solution)/shard_map/pallas_call | solution.py:324
  303.9 7.7 %fusion.39 = f32[3072,256]{1,0:T(8,128)} fusion(bf16[3072,3072]{1,0:T(8,128)(2,1)S(1)} %bitcast.27, bf16[3072,128]{1,0:T(8,128)(2,1)S(1)} %get-tuple-element.9, bf16[3072,128]{1,0:T(8,128)(2,1)S(1)} %get-tuple-element.10), kind=kOutput, calls=%fused_computation.53 | convolution fusion | flops 4834983936 | bytes 23592960 | tf_op jit(solution)/shard_map/dot_general | solution.py:386
  311.6 15.3 %fusion.15 = f32[3072,128]{1,0:T(8,128)S(1)} fusion(bf16[3072,128]{1,0:T(8,128)(2,1)S(1)} %get-tuple-element.10, f32[3072,3072]{1,0:T(8,128)} %get-tuple-element.18, f32[3072,256]{1,0:T(8,128)} %fusion.39), kind=kOutput, calls=%fused_computation.20 | convolution fusion | flops 2445017088 | bytes 43253760 | tf_op jit(solution)/shard_map/dot_general | solution.py:394
  327.0 29.9 %shard_map.60 = f32[768,128]{1,0:T(8,128)S(1)} custom-call(f32[4,768,128]{2,1,0:T(8,128)S(1)} %bitcast.23), custom_call_target="tpu_custom_call" | custom-call | tf_op jit(solution)/shard_map/pallas_call | solution.py:203
  356.9 0.8 multiply_subtract_fusion
  (40 shorter events, 1.9 us)
Async XLA Ops:
  6.5 105.4 %all-gather.5.cloned.1.call-start = ((), (), s32[]{:S(2)}) async-start(), calls=%async_computation.1 | async-start | bytes 1966080 | tf_op jit(solution)/shard_map/all_gather | solution.py:405
  7.3 107.5 %all-gather.3.cloned.1.call-start = ((), (), s32[]{:S(2)}) async-start(), calls=%async_computation | async-start | bytes 3932160 | tf_op jit(solution)/shard_map/all_gather | solution.py:356
  10.1 84.5 %copy-start.4 = (s32[768]{0:T(1024)S(1)}, s32[768]{0:T(1024)}, u32[]{:S(2)}) copy-start(s32[768]{0:T(1024)} %param.7) | copy-start | bytes 9220
  10.1 84.5 %copy-start.5 = (f32[16]{0:T(128)S(1)}, f32[16]{0:T(128)}, u32[]{:S(2)}) copy-start(f32[16]{0:T(128)} %param.8) | copy-start | bytes 196
  12.4 1.1 copy-start
  96.2 0.7 copy-start.3
  155.1 10.7 %copy-start.2 = (bf16[3072,128]{1,0:T(8,128)(2,1)S(1)}, bf16[3072,128]{1,0:T(8,128)(2,1)}, u32[]{:S(2)}) copy-start(bf16[3072,128]{1,0:T(8,128)(2,1)} %get-tuple-element.16) | copy-start | bytes 2359300
  205.9 67.4 %slice-start = ((s8[18874368]{0:T(1024)(128)(4,1)}), s8[4194304]{0:T(1024)(128)(4,1)S(1)}, s32[]{:S(2)}) async-start(s8[18874368]{0:T(1024)(128)(4,1)} %bitcast.26), calls=%async_computation.2 | async-start | bytes 8388608
  205.9 67.4 %slice-start.1 = ((s8[18874368]{0:T(1024)(128)(4,1)}), s8[4194304]{0:T(1024)(128)(4,1)S(1)}, s32[]{:S(2)}) async-start(s8[18874368]{0:T(1024)(128)(4,1)} %bitcast.26), calls=%async_computation.3 | async-start | bytes 8388608
  205.9 67.4 %slice-start.2 = ((s8[18874368]{0:T(1024)(128)(4,1)}), s8[4194304]{0:T(1024)(128)(4,1)S(1)}, s32[]{:S(2)}) async-start(s8[18874368]{0:T(1024)(128)(4,1)} %bitcast.26), calls=%async_computation.4 | async-start | bytes 8388608
  205.9 67.4 %slice-start.3 = ((s8[18874368]{0:T(1024)(128)(4,1)}), s8[4194304]{0:T(1024)(128)(4,1)S(1)}, s32[]{:S(2)}) async-start(s8[18874368]{0:T(1024)(128)(4,1)} %bitcast.26), calls=%async_computation.5 | async-start | bytes 8388608
  215.6 31.1 %copy-start.1 = (f32[768,128]{1,0:T(8,128)S(1)}, f32[768,128]{1,0:T(8,128)}, u32[]{:S(2)}) copy-start(f32[768,128]{1,0:T(8,128)} %param.6) | copy-start | bytes 1179652
  215.6 57.7 %slice-start.4 = ((s8[18874368]{0:T(1024)(128)(4,1)}), s8[2097152]{0:T(1024)(128)(4,1)S(1)}, s32[]{:S(2)}) async-start(s8[18874368]{0:T(1024)(128)(4,1)} %bitcast.26), calls=%async_computation.6 | async-start | bytes 4194304
Sparse Core Ops, SparseCore 0:
  8.9 53.2 all-gather.4
  63.8 27.0 all-gather.2

commit v3 on v2

--- a/solution.py
+++ b/solution.py
@@ -355,17 +355,26 @@
     weight_own = damping * damping
     z_rows = lax.all_gather(z_own, "col", axis=0, tiled=True)
     z_cols = line_gather(z_own, n_row, 0)
+    z_cols, vectors = lax.optimization_barrier((z_cols, vectors))
     tile_rows, tile_cols = z_rows.shape[0], z_cols.shape[0]
     blocks = removed_blocks.shape[0]
     block_size = order // blocks
-    row_block = (row_id * tile_rows + jnp.arange(tile_rows, dtype=jnp.int32)) // block_size
+    row_blocks = tile_rows // block_size
     position = jnp.arange(tile_cols, dtype=jnp.int32)
     col_index = (position // shard_rows * n_col + col_id) * shard_rows + position % shard_rows
     col_block = col_index // block_size
-    keep = (1 - removed_blocks).astype(jnp.bfloat16)
-    row_hot = (row_block[:, None] == jnp.arange(blocks)[None, :]).astype(jnp.bfloat16)
-    col_hot = (col_block[:, None] == jnp.arange(blocks)[None, :]).astype(jnp.bfloat16)
-    keep_rows = jnp.dot(row_hot, keep, preferred_element_type=jnp.float32).astype(jnp.bfloat16)
+    keep_rows = 1.0 - lax.dynamic_slice_in_dim(
+        removed_blocks, row_id * row_blocks, row_blocks, 0
+    ).astype(jnp.float32)
+    col_hot = (col_block[None, :] == jnp.arange(blocks, dtype=jnp.int32)[:, None]).astype(
+        jnp.float32
+    )
+    keep_small = jnp.dot(
+        keep_rows, col_hot, precision=lax.Precision.HIGHEST, preferred_element_type=jnp.float32
+    )
+    keep_full = jnp.broadcast_to(
+        keep_small[:, None, :], (row_blocks, block_size, tile_cols)
+    ).reshape(tile_rows, tile_cols)
     rows_high, rows_low = split(z_rows)
     cols_high, cols_low = split(z_cols * (sharpness / samples))
     scores = lax.dot_general(
@@ -373,9 +382,6 @@
         jnp.concatenate([cols_high, cols_high, cols_low], axis=1),
         (((1,), (1,)), ((), ())),
         preferred_element_type=jnp.float32,
-    )
-    keep_full = lax.dot_general(
-        keep_rows, col_hot, (((1,), (1,)), ((), ())), preferred_element_type=jnp.float32
     )
     t_high, t_low = split(jnp.tanh(scores) * keep_full)
     spectral_scale = 0.5 * order * jnp.mean(damp_levels * damp_levels)
@@ -389,9 +395,14 @@
             dims,
             preferred_element_type=jnp.float32,
         )
+        if fine:
+            both = both + lax.dot_general(
+                t_low,
+                jnp.concatenate([high, low], axis=1),
+                dims,
+                preferred_element_type=jnp.float32,
+            )
         out = both[:, :wide] + both[:, wide:]
-        if fine:
-            out = out + lax.dot_general(t_low, high, dims, preferred_element_type=jnp.float32)
         return out
 
     weight_wide = jnp.broadcast_to(weight_own[:, None], (shard_rows, wide))

time: 365 us -> 369 us (1.011)
  waiting for transfers between devices: 0.73 us -> 58.6 us
  matrix products: 116 us -> 81.2 us
  Pallas kernels: 217 us -> 193 us
    all_gather x1, waiting for transfers between devices: 0.01 us -> 31.8 us  [local(): vectors_cols = lax.all_gather(vectors, 'row', axis=0, tiled=True)]
    dot_general x3, matrix products: 45.5 us -> 15.8 us  [the longest x2 14.9 us: multiply(): lax.dot_general(t_low, jnp.concatenate([high, low], axis=1), dims, prefer...]
    all_gather x1, waiting for transfers between devices: 0.01 us -> 26.1 us  [local(): z_rows = lax.all_gather(z_own, 'col', axis=0, tiled=True)]
    pallas_call x2, Pallas kernels: 107 us -> 82.9 us  [line_gather(): pl.pallas_call(functools.partial(line_gather_kernel, n), out_shape=jax.Sh...]
    dot_general x1, matrix products: 36.3 us -> 25.3 us  [local(): lax.dot_general(jnp.concatenate([rows_high, rows_low, rows_high], axis=1)...]
    dot_general x4, matrix products: 33.8 us -> 40.1 us  [multiply(): lax.dot_general(t_high, jnp.concatenate([high, low], axis=1), dims, prefe...]
  transfers between devices with their start and end apart: 2 -> 2, of which waited for: 0 -> 2; matrix products, arithmetic and copies ran while one was open for 7% -> 2% of each run, Pallas kernels for 22% -> 0%
where the time goes in v3:
time: 369 us
  Pallas kernels  193 us (52%)
  matrix products  81.2 us (22%)
  waiting for transfers between devices  58.6 us (16%)
  other arithmetic  17.1 us (5%)
  between operations  14.3 us (4%)
  local copies, waits for them, and re-layouts  4.37 us (1%)
    pallas_call x2, Pallas kernels, line_gather(): pl.pallas_call(functools.partial(line_gather_kernel, n), out_shape=jax.Sh...  82.9 us
    pallas_call x2, Pallas kernels, line_scatter(): pl.pallas_call(functools.partial(line_scatter_kernel, n), out_shape=jax.S...  61.8 us
    pallas_call x2, Pallas kernels, plane_sum(): pl.pallas_call(functools.partial(plane_sum_kernel, nx), out_shape=jax.Sha...  48.5 us
    dot_general x4, matrix products, multiply(): lax.dot_general(t_high, jnp.concatenate([high, low], axis=1), dims, prefe...  40.1 us
    all_gather x1, waiting for transfers between devices, local(): vectors_cols = lax.all_gather(vectors, 'row', axis=0, tiled=True)  31.8 us
    all_gather x1, waiting for transfers between devices, local(): z_rows = lax.all_gather(z_own, 'col', axis=0, tiled=True)  26.1 us
    dot_general x1, matrix products, local(): lax.dot_general(jnp.concatenate([rows_high, rows_low, rows_high], axis=1)...  25.3 us
    dot_general x2, matrix products, multiply(): lax.dot_general(t_low, jnp.concatenate([high, low], axis=1), dims, prefer...  14.9 us
  transfers between devices with their start and end apart: 2, of which 2 were waited for; matrix products, arithmetic and copies ran while one was open for 2% of the time, Pallas kernels for 0%

profile of v3, /device:TPU:0, one launch (start us, length us, event | category | flops | bytes accessed | tf_op | source)
XLA Modules:
  0.0 368.9 jit_solution(7560698324127383990)
XLA Ops:
  6.5 1.3 reduce_sum.36
  7.9 1.4 multiply_reduce_fusion
  9.3 2.4 subtract_multiply_fusion.own_ref
  11.7 1.1 copy-done
  12.9 57.1 %shard_map.55 = f32[4,768,256]{2,1,0:T(8,128)S(1)} custom-call(f32[768,256]{1,0:T(8,128)S(1)} %copy-done), custom_call_target="tpu_custom_call" | custom-call | tf_op jit(solution)/shard_map/pallas_call | solution.py:105
  72.2 0.9 fusion.28
  73.1 2.1 reduce-precision_convert_fusion.1
  75.2 31.8 %all-gather.5.cloned.1.call-done = f32[3072,128]{1,0:T(8,128)} async-done(((f32[768,128]{1,0:T(8,128)}), f32[3072,128]{1,0:T(8,128)}) %all-gather.5.cloned.1.call-update) | async-done | bytes 1572880 | tf_op jit(solution)/shard_map/all_gather | solution.py:416
  107.0 2.9 reduce-precision_convert_fusion.6
  109.9 26.1 %all-gather.3.cloned.1.call-done = f32[3072,256]{1,0:T(8,128)} async-done(((f32[768,256]{1,0:T(8,128)}), f32[3072,256]{1,0:T(8,128)}) %all-gather.3.cloned.1.call-update) | async-done | bytes 3145744 | tf_op jit(solution)/shard_map/all_gather | solution.py:356
  136.0 4.0 %fusion.12 = (bf16[3072,256]{1,0:T(8,128)(2,1)}, bf16[3072,256]{1,0:T(8,128)(2,1)}) fusion(f32[3072,256]{1,0:T(8,128)} %all-gather.3.cloned.1.call-done), kind=kLoop, calls=%fused_computation.21 | loop fusion | flops 3145728 | bytes 6291456 | tf_op jit(solution)/shard_map/convert_element_type | solution.py:22
  140.0 25.3 %fusion = (bf16[3072,3072]{1,0:T(8,128)(2,1)}, bf16[3072,3072]{1,0:T(8,128)(2,1)}) fusion(f32[8,3072]{1,0:T(8,128)S(1)} %fusion.28, bf16[3072,256]{1,0:T(8,128)(2,1)S(1)} %copy-done.3, bf16[3072,256]{1,0:T(8,128)(2,1)S(1)} %copy-done.2, bf16[3072,256]{1,0:T(8,128)(2,1)} %get-tuple-element.14, bf16[3072,256]{1,0:T(8,128)(2,1)} %get-tuple-element.13), kind=kOutput, calls=%fused_computation.2 | convolution fusion | flops 14571012096 | bytes 44138496 | tf_op jit(solution)/shard_map/dot_general | solution.py:380
  165.3 10.8 %fusion.27 = f32[3072,256]{1,0:T(8,128)} fusion(bf16[3072,3072]{1,0:T(8,128)(2,1)} %get-tuple-element.10, bf16[3072,128]{1,0:T(8,128)(2,1)} %get-tuple-element.22, bf16[3072,128]{1,0:T(8,128)(2,1)} %get-tuple-element.21), kind=kOutput, calls=%fused_computation.50 | convolution fusion | flops 4834983936 | bytes 23592960 | tf_op jit(solution)/shard_map/dot_general | solution.py:392
  176.1 3.0 copy-done.8
  179.1 7.3 %convolution_add_fusion.1 = f32[3072,256]{1,0:T(8,128)S(1)} fusion(f32[3072,256]{1,0:T(8,128)} %fusion.27, bf16[3072,3072]{1,0:T(8,128)(2,1)S(1)} %copy-done.8, bf16[3072,128]{1,0:T(8,128)(2,1)S(1)} %copy-done.5, bf16[3072,128]{1,0:T(8,128)(2,1)S(1)} %copy-done.4), kind=kOutput, calls=%fused_computation.20 | convolution fusion | flops 4835770368 | bytes 26738688 | tf_op jit(solution)/shard_map/dot_general | solution.py:399
  186.8 24.1 %shard_map.56 = f32[2,2,768,128]{3,2,1,0:T(8,128)S(1)} custom-call(f32[2,2,768,128]{3,2,1,0:T(8,128)S(1)} %bitcast.27, f32[768,128]{1,0:T(8,128)S(1)} %broadcast_in_dim.5.weight_ref), custom_call_target="tpu_custom_call" | custom-call | tf_op jit(solution)/shard_map/pallas_call | solution.py:324
  211.1 9.1 %fusion.18 = f32[3072,256]{1,0:T(8,128)S(1)} fusion(bf16[3072,3072]{1,0:T(8,128)(2,1)} %get-tuple-element.10, bf16[3072,128]{1,0:T(8,128)(2,1)S(1)} %get-tuple-element.20, bf16[3072,128]{1,0:T(8,128)(2,1)S(1)} %get-tuple-element.19), kind=kOutput, calls=%fused_computation.40 | convolution fusion | flops 4834983936 | bytes 23592960 | tf_op jit(solution)/shard_map/dot_general | solution.py:392
  220.4 31.6 %shard_map.57 = f32[768,128]{1,0:T(8,128)S(1)} custom-call(f32[4,768,128]{2,1,0:T(8,128)S(1)} %bitcast.29), custom_call_target="tpu_custom_call" | custom-call | tf_op jit(solution)/shard_map/pallas_call | solution.py:203
  252.1 25.8 %shard_map.58 = f32[4,768,128]{2,1,0:T(8,128)S(1)} custom-call(f32[768,128]{1,0:T(8,128)S(1)} %divide_subtract_fusion.own_ref), custom_call_target="tpu_custom_call" | custom-call | tf_op jit(solution)/shard_map/pallas_call | solution.py:105
  278.2 9.2 %fusion.22 = f32[3072,256]{1,0:T(8,128)S(1)} fusion(bf16[3072,3072]{1,0:T(8,128)(2,1)} %get-tuple-element.10, bf16[3072,128]{1,0:T(8,128)(2,1)S(1)} %get-tuple-element.18, bf16[3072,128]{1,0:T(8,128)(2,1)S(1)} %get-tuple-element.17), kind=kOutput, calls=%fused_computation.44 | convolution fusion | flops 4834983936 | bytes 23592960 | tf_op jit(solution)/shard_map/dot_general | solution.py:392
  287.7 24.4 %shard_map.59 = f32[2,2,768,128]{3,2,1,0:T(8,128)S(1)} custom-call(f32[2,2,768,128]{3,2,1,0:T(8,128)S(1)} %bitcast.28, f32[768,128]{1,0:T(8,128)S(1)} %broadcast_in_dim.5.weight_ref), custom_call_target="tpu_custom_call" | custom-call | tf_op jit(solution)/shard_map/pallas_call | solution.py:324
  312.4 10.9 %fusion.26 = f32[3072,256]{1,0:T(8,128)} fusion(bf16[3072,3072]{1,0:T(8,128)(2,1)} %get-tuple-element.10, bf16[3072,128]{1,0:T(8,128)(2,1)S(1)} %get-tuple-element.16, bf16[3072,128]{1,0:T(8,128)(2,1)S(1)} %get-tuple-element.15), kind=kOutput, calls=%fused_computation.49 | convolution fusion | flops 4834983936 | bytes 23592960 | tf_op jit(solution)/shard_map/dot_general | solution.py:392
  323.3 7.6 %convolution_add_fusion = f32[3072,256]{1,0:T(8,128)S(1)} fusion(f32[3072,256]{1,0:T(8,128)} %fusion.26, bf16[3072,3072]{1,0:T(8,128)(2,1)S(1)} %copy-done.8, bf16[3072,128]{1,0:T(8,128)(2,1)S(1)} %get-tuple-element.16, bf16[3072,128]{1,0:T(8,128)(2,1)S(1)} %get-tuple-element.15), kind=kOutput, calls=%fused_computation.19 | convolution fusion | flops 4835770368 | bytes 26738688 | tf_op jit(solution)/shard_map/dot_general | solution.py:399
  331.0 30.1 %shard_map.60 = f32[768,128]{1,0:T(8,128)S(1)} custom-call(f32[4,768,128]{2,1,0:T(8,128)S(1)} %bitcast.30), custom_call_target="tpu_custom_call" | custom-call | tf_op jit(solution)/shard_map/pallas_call | solution.py:203
  (36 shorter events, 3.9 us)
Async XLA Ops:
  6.5 100.5 %all-gather.5.cloned.1.call-start = ((), (), s32[]{:S(2)}) async-start(), calls=%async_computation.1 | async-start | bytes 1966080 | tf_op jit(solution)/shard_map/all_gather | solution.py:416
  9.3 61.5 %copy-start.6 = (s32[768]{0:T(1024)S(1)}, s32[768]{0:T(1024)}, u32[]{:S(2)}) copy-start(s32[768]{0:T(1024)} %param.7) | copy-start | bytes 9220
  9.3 61.5 %copy-start.7 = (f32[16]{0:T(128)S(1)}, f32[16]{0:T(128)}, u32[]{:S(2)}) copy-start(f32[16]{0:T(128)} %param.8) | copy-start | bytes 196
  11.7 1.1 copy-start
  70.0 66.0 %all-gather.3.cloned.1.call-start = ((), (), s32[]{:S(2)}) async-start(), calls=%async_computation | async-start | bytes 3932160 | tf_op jit(solution)/shard_map/all_gather | solution.py:356
  109.9 30.1 %copy-start.2 = (bf16[3072,256]{1,0:T(8,128)(2,1)S(1)}, bf16[3072,256]{1,0:T(8,128)(2,1)}, u32[]{:S(2)}) copy-start(bf16[3072,256]{1,0:T(8,128)(2,1)} %get-tuple-element.11) | copy-start | bytes 4718596
  109.9 30.1 %copy-start.3 = (bf16[3072,256]{1,0:T(8,128)(2,1)S(1)}, bf16[3072,256]{1,0:T(8,128)(2,1)}, u32[]{:S(2)}) copy-start(bf16[3072,256]{1,0:T(8,128)(2,1)} %get-tuple-element.12) | copy-start | bytes 4718596
  165.3 10.8 %copy-start.4 = (bf16[3072,128]{1,0:T(8,128)(2,1)S(1)}, bf16[3072,128]{1,0:T(8,128)(2,1)}, u32[]{:S(2)}) copy-start(bf16[3072,128]{1,0:T(8,128)(2,1)} %get-tuple-element.21) | copy-start | bytes 2359300
  165.3 10.8 %copy-start.5 = (bf16[3072,128]{1,0:T(8,128)(2,1)S(1)}, bf16[3072,128]{1,0:T(8,128)(2,1)}, u32[]{:S(2)}) copy-start(bf16[3072,128]{1,0:T(8,128)(2,1)} %get-tuple-element.22) | copy-start | bytes 2359300
  165.3 13.8 %copy-start.8 = (bf16[3072,3072]{1,0:T(8,128)(2,1)S(1)}, bf16[3072,3072]{1,0:T(8,128)(2,1)}, u32[]{:S(2)}) copy-start(bf16[3072,3072]{1,0:T(8,128)(2,1)} %get-tuple-element.9) | copy-start | bytes 56623108
  220.3 31.8 %copy-start.1 = (f32[768,128]{1,0:T(8,128)S(1)}, f32[768,128]{1,0:T(8,128)}, u32[]{:S(2)}) copy-start(f32[768,128]{1,0:T(8,128)} %param.6) | copy-start | bytes 1179652
Sparse Core Ops, SparseCore 0:
  70.1 36.8 all-gather.4
  108.6 27.3 all-gather.2

commit v4 on v3

--- a/solution.py
+++ b/solution.py
@@ -112,6 +112,128 @@
             collective_id=collective_id, has_side_effects=True, vmem_limit_bytes=32 * 2**20
         ),
     )(own).reshape(n * rows, wide)
+
+
+def cross_gather_kernel(
+    n, nx, own_ref, cols_ref, rows_ref, send_right, recv_right, send_left, recv_left, *sems
+):
+    send_peer, recv_peer, send_core, recv_core = sems
+    me, col = lax.axis_index("row"), lax.axis_index("col")
+    core, x = col % 2, col // 2
+    partner = x * 2 + 1 - core
+    peers = [lax.rem(x + step, nx) * 2 + core for step in range(1, nx)]
+    barrier = pltpu.get_barrier_semaphore()
+    for device in [partner] + peers:
+        pl.semaphore_signal(barrier, inc=1, device_id={"col": device}, device_id_type=MESH)
+
+    @pl.when(me > 0)
+    def _():
+        pl.semaphore_signal(barrier, inc=1, device_id={"row": me - 1}, device_id_type=MESH)
+
+    @pl.when(me < n - 1)
+    def _():
+        pl.semaphore_signal(barrier, inc=1, device_id={"row": me + 1}, device_id_type=MESH)
+
+    inside = (me > 0) & (me < n - 1)
+
+    @pl.when(inside)
+    def _():
+        pl.semaphore_wait(barrier, nx + 2)
+
+    @pl.when(jnp.logical_not(inside))
+    def _():
+        pl.semaphore_wait(barrier, nx + 1)
+
+    cols_ref[me] = own_ref[...]
+    rows_ref[x, core] = own_ref[...]
+
+    def right(block, step, device):
+        place = cols_ref.at[block]
+        return send(place, place, send_right.at[step], recv_right.at[step], {"row": device})
+
+    def left(block, step, device):
+        place = cols_ref.at[block]
+        return send(place, place, send_left.at[step], recv_left.at[step], {"row": device})
+
+    copies = []
+    for step in range(n - 1):
+
+        @pl.when((me - step >= 0) & (me < n - 1))
+        def _():
+            right(me - step, step, me + 1).start()
+
+        @pl.when((me + step < n) & (me > 0))
+        def _():
+            left(me + step, step, me - 1).start()
+
+        if step == 0:
+            own = rows_ref.at[x, core]
+            for hop in range(1, nx):
+                copies.append(
+                    send(
+                        own,
+                        own,
+                        send_peer.at[hop - 1],
+                        recv_peer.at[hop - 1],
+                        {"col": peers[hop - 1]},
+                    )
+                )
+                copies[-1].start()
+            copies.append(send(own, own, send_core.at[0], recv_core.at[0], {"col": partner}))
+            copies[-1].start()
+
+        @pl.when(me - 1 - step >= 0)
+        def _():
+            right(me - 1 - step, step, me - 1).wait_recv()
+
+        @pl.when(me + 1 + step < n)
+        def _():
+            left(me + 1 + step, step, me + 1).wait_recv()
+
+    for hop in range(1, nx):
+        origin = lax.rem(x + nx - hop, nx)
+        place = rows_ref.at[origin, core]
+        send(
+            place, place, send_peer.at[hop - 1], recv_peer.at[hop - 1], {"col": origin * 2 + core}
+        ).wait_recv()
+        copies.append(send(place, place, send_core.at[hop], recv_core.at[hop], {"col": partner}))
+        copies[-1].start()
+    for hop in range(nx):
+        place = rows_ref.at[lax.rem(x + nx - hop, nx), 1 - core]
+        send(place, place, send_core.at[hop], recv_core.at[hop], {"col": partner}).wait_recv()
+    for copy in copies:
+        copy.wait_send()
+    for step in range(n - 1):
+
+        @pl.when((me - step >= 0) & (me < n - 1))
+        def _():
+            right(me - step, step, me + 1).wait_send()
+
+        @pl.when((me + step < n) & (me > 0))
+        def _():
+            left(me + step, step, me - 1).wait_send()
+
+
+def cross_gather(own, n, n_col, collective_id):
+    nx = n_col // 2
+    rows, wide = own.shape
+    by_row, by_col = pl.pallas_call(
+        functools.partial(cross_gather_kernel, n, nx),
+        out_shape=(
+            jax.ShapeDtypeStruct((n, rows, wide), own.dtype),
+            jax.ShapeDtypeStruct((nx, 2, rows, wide), own.dtype),
+        ),
+        in_specs=[pl.BlockSpec(memory_space=pltpu.VMEM)],
+        out_specs=(
+            pl.BlockSpec(memory_space=pltpu.VMEM),
+            pl.BlockSpec(memory_space=pltpu.VMEM),
+        ),
+        scratch_shapes=[pltpu.SemaphoreType.DMA((n - 1,))] * 4 + plane_sems(nx),
+        compiler_params=pltpu.CompilerParams(
+            collective_id=collective_id, has_side_effects=True, vmem_limit_bytes=32 * 2**20
+        ),
+    )(own)
+    return by_row.reshape(n * rows, wide), by_col.reshape(n_col * rows, wide)
 
 
 def line_scatter_kernel(
@@ -353,8 +475,7 @@
     )
     damping = jnp.sum(onehot * damp_levels[None, :], axis=1)
     weight_own = damping * damping
-    z_rows = lax.all_gather(z_own, "col", axis=0, tiled=True)
-    z_cols = line_gather(z_own, n_row, 0)
+    z_cols, z_rows = cross_gather(z_own, n_row, n_col, 0)
     z_cols, vectors = lax.optimization_barrier((z_cols, vectors))
     tile_rows, tile_cols = z_rows.shape[0], z_cols.shape[0]
     blocks = removed_blocks.shape[0]
@@ -414,6 +535,7 @@
         return line_scatter(returned, n_row, 3) / spectral_scale
 
     vectors_cols = lax.all_gather(vectors, "row", axis=0, tiled=True)
+    vectors_cols, t_high, t_low = lax.optimization_barrier((vectors_cols, t_high, t_low))
     first_term = normal_apply(vectors_cols, (True, False)) - vectors
     first_cols = line_gather(first_term, n_row, 1)
     return 2.0 * (normal_apply(first_cols, (False, True)) - first_term) - vectors

time: 369 us -> 312 us (0.85)
  waiting for transfers between devices: 58.6 us -> 1.72 us
    pallas_call x0 -> x1, Pallas kernels: none -> 59.8 us  [cross_gather(): pl.pallas_call(functools.partial(cross_gather_kernel, n, nx), out_shape=(...]
    pallas_call x2 -> x1, Pallas kernels: 82.9 us -> 25.8 us  [line_gather(): pl.pallas_call(functools.partial(line_gather_kernel, n), out_shape=jax.Sh...]
    all_gather x1, waiting for transfers between devices: 31.8 us -> 1.7 us  [local(): vectors_cols = lax.all_gather(vectors, 'row', axis=0, tiled=True)]
    all_gather x1 -> x0, waiting for transfers between devices: 26.1 us -> none  [local(): z_rows = lax.all_gather(z_own, 'col', axis=0, tiled=True)]
  transfers between devices with their start and end apart: 2 -> 1, of which waited for: 2 -> 1; matrix products, arithmetic and copies ran while one was open for 2% -> 11% of each run, Pallas kernels for 0% -> 0%
where the time goes in v4:
time: 312 us
  Pallas kernels  196 us (63%)
  matrix products  82.1 us (26%)
  other arithmetic  15.2 us (5%)
  between operations  14.3 us (5%)
    pallas_call x2, Pallas kernels, line_scatter(): pl.pallas_call(functools.partial(line_scatter_kernel, n), out_shape=jax.S...  60.6 us
    pallas_call x1, Pallas kernels, cross_gather(): pl.pallas_call(functools.partial(cross_gather_kernel, n, nx), out_shape=(...  59.8 us
    pallas_call x2, Pallas kernels, plane_sum(): pl.pallas_call(functools.partial(plane_sum_kernel, nx), out_shape=jax.Sha...  49.3 us
    dot_general x4, matrix products, multiply(): lax.dot_general(t_high, jnp.concatenate([high, low], axis=1), dims, prefe...  40.1 us
    dot_general x1, matrix products, local(): lax.dot_general(jnp.concatenate([rows_high, rows_low, rows_high], axis=1)...  26.3 us
    pallas_call x1, Pallas kernels, line_gather(): pl.pallas_call(functools.partial(line_gather_kernel, n), out_shape=jax.Sh...  25.8 us
    dot_general x2, matrix products, multiply(): lax.dot_general(t_low, jnp.concatenate([high, low], axis=1), dims, prefer...  14.9 us
    convert_element_type x6, other arithmetic, split(): return (high.astype(jnp.bfloat16), (x - high).astype(jnp.bfloat16))  8.85 us
  transfers between devices with their start and end apart: 1, of which 1 were waited for; matrix products, arithmetic and copies ran while one was open for 11% of the time, Pallas kernels for 0%

profile of v4, /device:TPU:0, one launch (start us, length us, event | category | flops | bytes accessed | tf_op | source)
XLA Modules:
  0.0 311.6 jit_solution(15358375853952206068)
XLA Ops:
  6.5 1.3 reduce_sum.36
  7.9 1.4 multiply_reduce_fusion
  9.3 1.4 subtract_multiply_fusion.own_ref
  10.7 59.8 %shard_map.55 = (f32[4,768,256]{2,1,0:T(8,128)S(1)}, f32[2,2,768,256]{3,2,1,0:T(8,128)S(1)}) custom-call(f32[768,256]{1,0:T(8,128)S(1)} %subtract_multiply_fusion.own_ref), custom_call_target="tpu_custom_call" | custom-call | tf_op jit(solution)/shard_map/pallas_call | solution.py:220
  70.6 1.6 copy-done
  73.7 0.9 fusion.28
  74.6 4.1 %reduce-precision_convert_fusion.1 = (bf16[3072,256]{1,0:T(8,128)(2,1)}, bf16[3072,256]{1,0:T(8,128)(2,1)}) fusion(f32[3072,256]{1,0:T(8,128)} %bitcast.33), kind=kLoop, calls=%fused_computation.16 | loop fusion | flops 3932160 | bytes 6291456 | tf_op jit(solution)/shard_map/convert_element_type | solution.py:22
  78.7 2.2 fusion.12
  80.9 26.3 %fusion = (bf16[3072,3072]{1,0:T(8,128)(2,1)}, bf16[3072,3072]{1,0:T(8,128)(2,1)}) fusion(f32[8,3072]{1,0:T(8,128)S(1)} %fusion.28, bf16[3072,256]{1,0:T(8,128)(2,1)} %get-tuple-element.22, bf16[3072,256]{1,0:T(8,128)(2,1)} %get-tuple-element.21, bf16[3072,256]{1,0:T(8,128)(2,1)} %get-tuple-element.24, bf16[3072,256]{1,0:T(8,128)(2,1)} %get-tuple-element.23), kind=kOutput, calls=%fused_computation.2 | convolution fusion | flops 14571012096 | bytes 44138496 | tf_op jit(solution)/shard_map/dot_general | solution.py:501
  107.1 1.7 all-gather.2.cloned.1.call-done
  108.8 1.8 reduce-precision_convert_fusion.6
  110.7 10.8 %fusion.27 = f32[3072,256]{1,0:T(8,128)} fusion(bf16[3072,3072]{1,0:T(8,128)(2,1)} %get-tuple-element.16, bf16[3072,128]{1,0:T(8,128)(2,1)S(1)} %get-tuple-element.32, bf16[3072,128]{1,0:T(8,128)(2,1)S(1)} %get-tuple-element.31), kind=kOutput, calls=%fused_computation.50 | convolution fusion | flops 4834983936 | bytes 23592960 | tf_op jit(solution)/shard_map/dot_general | solution.py:513
  121.5 0.8 slice-done.4
  122.3 7.3 %convolution_add_fusion.1 = f32[3072,256]{1,0:T(8,128)S(1)} fusion(f32[3072,256]{1,0:T(8,128)} %fusion.27, bf16[3072,3072]{1,0:T(8,128)(2,1)S(1)} %bitcast.35, bf16[3072,128]{1,0:T(8,128)(2,1)S(1)} %get-tuple-element.32, bf16[3072,128]{1,0:T(8,128)(2,1)S(1)} %get-tuple-element.31), kind=kOutput, calls=%fused_computation.20 | convolution fusion | flops 4835770368 | bytes 26738688 | tf_op jit(solution)/shard_map/dot_general | solution.py:520
  130.0 24.8 %shard_map.56 = f32[2,2,768,128]{3,2,1,0:T(8,128)S(1)} custom-call(f32[2,2,768,128]{3,2,1,0:T(8,128)S(1)} %bitcast.29, f32[768,128]{1,0:T(8,128)S(1)} %broadcast_in_dim.5.weight_ref), custom_call_target="tpu_custom_call" | custom-call | tf_op jit(solution)/shard_map/pallas_call | solution.py:446
  155.1 9.1 %fusion.18 = f32[3072,256]{1,0:T(8,128)S(1)} fusion(bf16[3072,3072]{1,0:T(8,128)(2,1)} %get-tuple-element.16, bf16[3072,128]{1,0:T(8,128)(2,1)S(1)} %get-tuple-element.30, bf16[3072,128]{1,0:T(8,128)(2,1)S(1)} %get-tuple-element.29), kind=kOutput, calls=%fused_computation.40 | convolution fusion | flops 4834983936 | bytes 23592960 | tf_op jit(solution)/shard_map/dot_general | solution.py:513
  164.3 30.3 %shard_map.57 = f32[768,128]{1,0:T(8,128)S(1)} custom-call(f32[4,768,128]{2,1,0:T(8,128)S(1)} %bitcast.31), custom_call_target="tpu_custom_call" | custom-call | tf_op jit(solution)/shard_map/pallas_call | solution.py:325
  194.7 25.8 %shard_map.58 = f32[4,768,128]{2,1,0:T(8,128)S(1)} custom-call(f32[768,128]{1,0:T(8,128)S(1)} %divide_subtract_fusion.own_ref), custom_call_target="tpu_custom_call" | custom-call | tf_op jit(solution)/shard_map/pallas_call | solution.py:105
  220.8 9.2 %fusion.22 = f32[3072,256]{1,0:T(8,128)S(1)} fusion(bf16[3072,3072]{1,0:T(8,128)(2,1)} %get-tuple-element.16, bf16[3072,128]{1,0:T(8,128)(2,1)S(1)} %get-tuple-element.28, bf16[3072,128]{1,0:T(8,128)(2,1)S(1)} %get-tuple-element.27), kind=kOutput, calls=%fused_computation.44 | convolution fusion | flops 4834983936 | bytes 23592960 | tf_op jit(solution)/shard_map/dot_general | solution.py:513
  230.2 24.5 %shard_map.59 = f32[2,2,768,128]{3,2,1,0:T(8,128)S(1)} custom-call(f32[2,2,768,128]{3,2,1,0:T(8,128)S(1)} %bitcast.30, f32[768,128]{1,0:T(8,128)S(1)} %broadcast_in_dim.5.weight_ref), custom_call_target="tpu_custom_call" | custom-call | tf_op jit(solution)/shard_map/pallas_call | solution.py:446
  254.9 11.0 %fusion.26 = f32[3072,256]{1,0:T(8,128)} fusion(bf16[3072,3072]{1,0:T(8,128)(2,1)} %get-tuple-element.16, bf16[3072,128]{1,0:T(8,128)(2,1)S(1)} %get-tuple-element.26, bf16[3072,128]{1,0:T(8,128)(2,1)S(1)} %get-tuple-element.25), kind=kOutput, calls=%fused_computation.49 | convolution fusion | flops 4834983936 | bytes 23592960 | tf_op jit(solution)/shard_map/dot_general | solution.py:513
  265.9 7.6 %convolution_add_fusion = f32[3072,256]{1,0:T(8,128)S(1)} fusion(f32[3072,256]{1,0:T(8,128)} %fusion.26, bf16[3072,3072]{1,0:T(8,128)(2,1)S(1)} %bitcast.35, bf16[3072,128]{1,0:T(8,128)(2,1)S(1)} %get-tuple-element.26, bf16[3072,128]{1,0:T(8,128)(2,1)S(1)} %get-tuple-element.25), kind=kOutput, calls=%fused_computation.19 | convolution fusion | flops 4835770368 | bytes 26738688 | tf_op jit(solution)/shard_map/dot_general | solution.py:520
  273.6 30.3 %shard_map.60 = f32[768,128]{1,0:T(8,128)S(1)} custom-call(f32[4,768,128]{2,1,0:T(8,128)S(1)} %bitcast.32), custom_call_target="tpu_custom_call" | custom-call | tf_op jit(solution)/shard_map/pallas_call | solution.py:325
  304.0 0.8 multiply_subtract_fusion
  (34 shorter events, 2.3 us)
Async XLA Ops:
  6.5 65.7 %copy-start.2 = (s32[768]{0:T(1024)S(1)}, s32[768]{0:T(1024)}, u32[]{:S(2)}) copy-start(s32[768]{0:T(1024)} %param.7) | copy-start | bytes 9220
  6.5 65.7 %copy-start.3 = (f32[16]{0:T(128)S(1)}, f32[16]{0:T(128)}, u32[]{:S(2)}) copy-start(f32[16]{0:T(128)} %param.8) | copy-start | bytes 196
  6.5 102.3 %all-gather.2.cloned.1.call-start = ((), (), s32[]{:S(2)}) async-start(), calls=%async_computation | async-start | bytes 1966080 | tf_op jit(solution)/shard_map/all_gather | solution.py:537
  70.6 1.6 copy-start
  108.8 12.6 %slice-start = ((s8[18874368]{0:T(1024)(128)(4,1)}), s8[4194304]{0:T(1024)(128)(4,1)S(1)}, s32[]{:S(2)}) async-start(s8[18874368]{0:T(1024)(128)(4,1)} %bitcast.34), calls=%async_computation.1 | async-start | bytes 8388608
  110.7 10.8 %slice-start.1 = ((s8[18874368]{0:T(1024)(128)(4,1)}), s8[4194304]{0:T(1024)(128)(4,1)S(1)}, s32[]{:S(2)}) async-start(s8[18874368]{0:T(1024)(128)(4,1)} %bitcast.34), calls=%async_computation.2 | async-start | bytes 8388608
  110.7 10.8 %slice-start.2 = ((s8[18874368]{0:T(1024)(128)(4,1)}), s8[4194304]{0:T(1024)(128)(4,1)S(1)}, s32[]{:S(2)}) async-start(s8[18874368]{0:T(1024)(128)(4,1)} %bitcast.34), calls=%async_computation.3 | async-start | bytes 8388608
  110.7 10.8 %slice-start.3 = ((s8[18874368]{0:T(1024)(128)(4,1)}), s8[4194304]{0:T(1024)(128)(4,1)S(1)}, s32[]{:S(2)}) async-start(s8[18874368]{0:T(1024)(128)(4,1)} %bitcast.34), calls=%async_computation.4 | async-start | bytes 8388608
  110.7 11.6 %slice-start.4 = ((s8[18874368]{0:T(1024)(128)(4,1)}), s8[2097152]{0:T(1024)(128)(4,1)S(1)}, s32[]{:S(2)}) async-start(s8[18874368]{0:T(1024)(128)(4,1)} %bitcast.34), calls=%async_computation.5 | async-start | bytes 4194304
  164.2 30.4 %copy-start.1 = (f32[768,128]{1,0:T(8,128)S(1)}, f32[768,128]{1,0:T(8,128)}, u32[]{:S(2)}) copy-start(f32[768,128]{1,0:T(8,128)} %param.6) | copy-start | bytes 1179652
Sparse Core Ops, SparseCore 0:
  72.4 36.4 all-gather.1

commit v5 on v4

--- a/solution.py
+++ b/solution.py
@@ -64,40 +64,54 @@
     out_ref[me] = own_ref[...]
 
     def right(block, step, device):
-        place = out_ref.at[block]
+        half = out_ref.shape[1] // 2
+        place = out_ref.at[block, pl.ds(step % 2 * half, half)]
         return send(place, place, send_right.at[step], recv_right.at[step], {"row": device})
 
     def left(block, step, device):
-        place = out_ref.at[block]
+        half = out_ref.shape[1] // 2
+        place = out_ref.at[block, pl.ds(step % 2 * half, half)]
         return send(place, place, send_left.at[step], recv_left.at[step], {"row": device})
 
-    for step in range(n - 1):
-
-        @pl.when((me - step >= 0) & (me < n - 1))
-        def _():
-            right(me - step, step, me + 1).start()
-
-        @pl.when((me + step < n) & (me > 0))
-        def _():
-            left(me + step, step, me - 1).start()
-
-        @pl.when(me - 1 - step >= 0)
-        def _():
-            right(me - 1 - step, step, me - 1).wait_recv()
-
-        @pl.when(me + 1 + step < n)
-        def _():
-            left(me + 1 + step, step, me + 1).wait_recv()
-
-    for step in range(n - 1):
-
-        @pl.when((me - step >= 0) & (me < n - 1))
-        def _():
-            right(me - step, step, me + 1).wait_send()
-
-        @pl.when((me + step < n) & (me > 0))
-        def _():
-            left(me + step, step, me - 1).wait_send()
+    for step in range(2 * n - 2):
+
+        if step >= 2:
+            done = step - 2
+            @pl.when(me - 1 - done // 2 >= 0)
+            def _():
+                right(me - 1 - done // 2, done, me - 1).wait_recv()
+
+            @pl.when(me + 1 + done // 2 < n)
+            def _():
+                left(me + 1 + done // 2, done, me + 1).wait_recv()
+
+        @pl.when((me - step // 2 >= 0) & (me < n - 1))
+        def _():
+            right(me - step // 2, step, me + 1).start()
+
+        @pl.when((me + step // 2 < n) & (me > 0))
+        def _():
+            left(me + step // 2, step, me - 1).start()
+
+    for done in range(2 * n - 4, 2 * n - 2):
+
+        @pl.when(me - 1 - done // 2 >= 0)
+        def _():
+            right(me - 1 - done // 2, done, me - 1).wait_recv()
+
+        @pl.when(me + 1 + done // 2 < n)
+        def _():
+            left(me + 1 + done // 2, done, me + 1).wait_recv()
+
+    for step in range(2 * n - 2):
+
+        @pl.when((me - step // 2 >= 0) & (me < n - 1))
+        def _():
+            right(me - step // 2, step, me + 1).wait_send()
+
+        @pl.when((me + step // 2 < n) & (me > 0))
+        def _():
+            left(me + step // 2, step, me - 1).wait_send()
 
 
 def line_gather(own, n, collective_id):
@@ -107,7 +121,7 @@
         out_shape=jax.ShapeDtypeStruct((n, rows, wide), own.dtype),
         in_specs=[pl.BlockSpec(memory_space=pltpu.VMEM)],
         out_specs=pl.BlockSpec(memory_space=pltpu.VMEM),
-        scratch_shapes=[pltpu.SemaphoreType.DMA((n - 1,))] * 4,
+        scratch_shapes=[pltpu.SemaphoreType.DMA((2 * n - 2,))] * 4,
         compiler_params=pltpu.CompilerParams(
             collective_id=collective_id, has_side_effects=True, vmem_limit_bytes=32 * 2**20
         ),
@@ -148,23 +162,35 @@
     rows_ref[x, core] = own_ref[...]
 
     def right(block, step, device):
-        place = cols_ref.at[block]
+        half = cols_ref.shape[1] // 2
+        place = cols_ref.at[block, pl.ds(step % 2 * half, half)]
         return send(place, place, send_right.at[step], recv_right.at[step], {"row": device})
 
     def left(block, step, device):
-        place = cols_ref.at[block]
+        half = cols_ref.shape[1] // 2
+        place = cols_ref.at[block, pl.ds(step % 2 * half, half)]
         return send(place, place, send_left.at[step], recv_left.at[step], {"row": device})
 
     copies = []
-    for step in range(n - 1):
-
-        @pl.when((me - step >= 0) & (me < n - 1))
-        def _():
-            right(me - step, step, me + 1).start()
-
-        @pl.when((me + step < n) & (me > 0))
-        def _():
-            left(me + step, step, me - 1).start()
+    for step in range(2 * n - 2):
+
+        if step >= 2:
+            done = step - 2
+            @pl.when(me - 1 - done // 2 >= 0)
+            def _():
+                right(me - 1 - done // 2, done, me - 1).wait_recv()
+
+            @pl.when(me + 1 + done // 2 < n)
+            def _():
+                left(me + 1 + done // 2, done, me + 1).wait_recv()
+
+        @pl.when((me - step // 2 >= 0) & (me < n - 1))
+        def _():
+            right(me - step // 2, step, me + 1).start()
+
+        @pl.when((me + step // 2 < n) & (me > 0))
+        def _():
+            left(me + step // 2, step, me - 1).start()
 
         if step == 0:
             own = rows_ref.at[x, core]
@@ -182,13 +208,15 @@
             copies.append(send(own, own, send_core.at[0], recv_core.at[0], {"col": partner}))
             copies[-1].start()
 
-        @pl.when(me - 1 - step >= 0)
-        def _():
-            right(me - 1 - step, step, me - 1).wait_recv()
-
-        @pl.when(me + 1 + step < n)
-        def _():
-            left(me + 1 + step, step, me + 1).wait_recv()
+    for done in range(2 * n - 4, 2 * n - 2):
+
+        @pl.when(me - 1 - done // 2 >= 0)
+        def _():
+            right(me - 1 - done // 2, done, me - 1).wait_recv()
+
+        @pl.when(me + 1 + done // 2 < n)
+        def _():
+            left(me + 1 + done // 2, done, me + 1).wait_recv()
 
     for hop in range(1, nx):
         origin = lax.rem(x + nx - hop, nx)
@@ -203,15 +231,15 @@
         send(place, place, send_core.at[hop], recv_core.at[hop], {"col": partner}).wait_recv()
     for copy in copies:
         copy.wait_send()
-    for step in range(n - 1):
-
-        @pl.when((me - step >= 0) & (me < n - 1))
-        def _():
-            right(me - step, step, me + 1).wait_send()
-
-        @pl.when((me + step < n) & (me > 0))
-        def _():
-            left(me + step, step, me - 1).wait_send()
+    for step in range(2 * n - 2):
+
+        @pl.when((me - step // 2 >= 0) & (me < n - 1))
+        def _():
+            right(me - step // 2, step, me + 1).wait_send()
+
+        @pl.when((me + step // 2 < n) & (me > 0))
+        def _():
+            left(me + step // 2, step, me - 1).wait_send()
 
 
 def cross_gather(own, n, n_col, collective_id):
@@ -228,7 +256,7 @@
             pl.BlockSpec(memory_space=pltpu.VMEM),
             pl.BlockSpec(memory_space=pltpu.VMEM),
         ),
-        scratch_shapes=[pltpu.SemaphoreType.DMA((n - 1,))] * 4 + plane_sems(nx),
+        scratch_shapes=[pltpu.SemaphoreType.DMA((2 * n - 2,))] * 4 + plane_sems(nx),
         compiler_params=pltpu.CompilerParams(
             collective_id=collective_id, has_side_effects=True, vmem_limit_bytes=32 * 2**20
         ),

time: 312 us -> 311 us (level)
  no operation moved by 1% of the time
where the time goes in v5:
time: 311 us
  Pallas kernels  194 us (62%)
  matrix products  82.1 us (26%)
  other arithmetic  15.2 us (5%)
  between operations  14.3 us (5%)
    pallas_call x2, Pallas kernels, line_scatter(): pl.pallas_call(functools.partial(line_scatter_kernel, n), out_shape=jax.S...  60.8 us
    pallas_call x1, Pallas kernels, cross_gather(): pl.pallas_call(functools.partial(cross_gather_kernel, n, nx), out_shape=(...  57.9 us
    pallas_call x2, Pallas kernels, plane_sum(): pl.pallas_call(functools.partial(plane_sum_kernel, nx), out_shape=jax.Sha...  49.3 us
    dot_general x4, matrix products, multiply(): lax.dot_general(t_high, jnp.concatenate([high, low], axis=1), dims, prefe...  40.1 us
    dot_general x1, matrix products, local(): lax.dot_general(jnp.concatenate([rows_high, rows_low, rows_high], axis=1)...  26.2 us
    pallas_call x1, Pallas kernels, line_gather(): pl.pallas_call(functools.partial(line_gather_kernel, n), out_shape=jax.Sh...  25.9 us
    dot_general x2, matrix products, multiply(): lax.dot_general(t_low, jnp.concatenate([high, low], axis=1), dims, prefer...  14.9 us
    convert_element_type x6, other arithmetic, split(): return (high.astype(jnp.bfloat16), (x - high).astype(jnp.bfloat16))  8.81 us
  transfers between devices with their start and end apart: 1, of which 1 were waited for; matrix products, arithmetic and copies ran while one was open for 11% of the time, Pallas kernels for 0%

profile of v5, /device:TPU:0, one launch (start us, length us, event | category | flops | bytes accessed | tf_op | source)
XLA Modules:
  0.0 310.8 jit_solution(10150425679715059447)
XLA Ops:
  6.5 1.3 reduce_sum.36
  7.9 1.4 multiply_reduce_fusion
  9.3 1.4 subtract_multiply_fusion.own_ref
  10.7 57.9 %shard_map.55 = (f32[4,768,256]{2,1,0:T(8,128)S(1)}, f32[2,2,768,256]{3,2,1,0:T(8,128)S(1)}) custom-call(f32[768,256]{1,0:T(8,128)S(1)} %subtract_multiply_fusion.own_ref), custom_call_target="tpu_custom_call" | custom-call | tf_op jit(solution)/shard_map/pallas_call | solution.py:248
  68.7 1.6 copy-done
  71.7 0.9 fusion.28
  72.7 4.0 %reduce-precision_convert_fusion.1 = (bf16[3072,256]{1,0:T(8,128)(2,1)}, bf16[3072,256]{1,0:T(8,128)(2,1)}) fusion(f32[3072,256]{1,0:T(8,128)} %bitcast.33), kind=kLoop, calls=%fused_computation.16 | loop fusion | flops 3932160 | bytes 6291456 | tf_op jit(solution)/shard_map/convert_element_type | solution.py:22
  76.7 2.2 fusion.12
  78.9 26.2 %fusion = (bf16[3072,3072]{1,0:T(8,128)(2,1)}, bf16[3072,3072]{1,0:T(8,128)(2,1)}) fusion(f32[8,3072]{1,0:T(8,128)S(1)} %fusion.28, bf16[3072,256]{1,0:T(8,128)(2,1)} %get-tuple-element.22, bf16[3072,256]{1,0:T(8,128)(2,1)} %get-tuple-element.21, bf16[3072,256]{1,0:T(8,128)(2,1)} %get-tuple-element.24, bf16[3072,256]{1,0:T(8,128)(2,1)} %get-tuple-element.23), kind=kOutput, calls=%fused_computation.2 | convolution fusion | flops 14571012096 | bytes 44138496 | tf_op jit(solution)/shard_map/dot_general | solution.py:529
  105.2 2.6 all-gather.2.cloned.1.call-done
  107.7 1.8 reduce-precision_convert_fusion.6
  109.6 10.8 %fusion.27 = f32[3072,256]{1,0:T(8,128)} fusion(bf16[3072,3072]{1,0:T(8,128)(2,1)} %get-tuple-element.16, bf16[3072,128]{1,0:T(8,128)(2,1)S(1)} %get-tuple-element.32, bf16[3072,128]{1,0:T(8,128)(2,1)S(1)} %get-tuple-element.31), kind=kOutput, calls=%fused_computation.50 | convolution fusion | flops 4834983936 | bytes 23592960 | tf_op jit(solution)/shard_map/dot_general | solution.py:541
  120.4 0.8 slice-done.4
  121.2 7.3 %convolution_add_fusion.1 = f32[3072,256]{1,0:T(8,128)S(1)} fusion(f32[3072,256]{1,0:T(8,128)} %fusion.27, bf16[3072,3072]{1,0:T(8,128)(2,1)S(1)} %bitcast.35, bf16[3072,128]{1,0:T(8,128)(2,1)S(1)} %get-tuple-element.32, bf16[3072,128]{1,0:T(8,128)(2,1)S(1)} %get-tuple-element.31), kind=kOutput, calls=%fused_computation.20 | convolution fusion | flops 4835770368 | bytes 26738688 | tf_op jit(solution)/shard_map/dot_general | solution.py:548
  128.8 24.8 %shard_map.56 = f32[2,2,768,128]{3,2,1,0:T(8,128)S(1)} custom-call(f32[2,2,768,128]{3,2,1,0:T(8,128)S(1)} %bitcast.29, f32[768,128]{1,0:T(8,128)S(1)} %broadcast_in_dim.5.weight_ref), custom_call_target="tpu_custom_call" | custom-call | tf_op jit(solution)/shard_map/pallas_call | solution.py:474
  153.9 9.1 %fusion.18 = f32[3072,256]{1,0:T(8,128)S(1)} fusion(bf16[3072,3072]{1,0:T(8,128)(2,1)} %get-tuple-element.16, bf16[3072,128]{1,0:T(8,128)(2,1)S(1)} %get-tuple-element.30, bf16[3072,128]{1,0:T(8,128)(2,1)S(1)} %get-tuple-element.29), kind=kOutput, calls=%fused_computation.40 | convolution fusion | flops 4834983936 | bytes 23592960 | tf_op jit(solution)/shard_map/dot_general | solution.py:541
  163.2 30.3 %shard_map.57 = f32[768,128]{1,0:T(8,128)S(1)} custom-call(f32[4,768,128]{2,1,0:T(8,128)S(1)} %bitcast.31), custom_call_target="tpu_custom_call" | custom-call | tf_op jit(solution)/shard_map/pallas_call | solution.py:353
  193.6 25.9 %shard_map.58 = f32[4,768,128]{2,1,0:T(8,128)S(1)} custom-call(f32[768,128]{1,0:T(8,128)S(1)} %divide_subtract_fusion.own_ref), custom_call_target="tpu_custom_call" | custom-call | tf_op jit(solution)/shard_map/pallas_call | solution.py:119
  219.8 9.2 %fusion.22 = f32[3072,256]{1,0:T(8,128)S(1)} fusion(bf16[3072,3072]{1,0:T(8,128)(2,1)} %get-tuple-element.16, bf16[3072,128]{1,0:T(8,128)(2,1)S(1)} %get-tuple-element.28, bf16[3072,128]{1,0:T(8,128)(2,1)S(1)} %get-tuple-element.27), kind=kOutput, calls=%fused_computation.44 | convolution fusion | flops 4834983936 | bytes 23592960 | tf_op jit(solution)/shard_map/dot_general | solution.py:541
  229.2 24.5 %shard_map.59 = f32[2,2,768,128]{3,2,1,0:T(8,128)S(1)} custom-call(f32[2,2,768,128]{3,2,1,0:T(8,128)S(1)} %bitcast.30, f32[768,128]{1,0:T(8,128)S(1)} %broadcast_in_dim.5.weight_ref), custom_call_target="tpu_custom_call" | custom-call | tf_op jit(solution)/shard_map/pallas_call | solution.py:474
  253.9 11.0 %fusion.26 = f32[3072,256]{1,0:T(8,128)} fusion(bf16[3072,3072]{1,0:T(8,128)(2,1)} %get-tuple-element.16, bf16[3072,128]{1,0:T(8,128)(2,1)S(1)} %get-tuple-element.26, bf16[3072,128]{1,0:T(8,128)(2,1)S(1)} %get-tuple-element.25), kind=kOutput, calls=%fused_computation.49 | convolution fusion | flops 4834983936 | bytes 23592960 | tf_op jit(solution)/shard_map/dot_general | solution.py:541
  264.9 7.6 %convolution_add_fusion = f32[3072,256]{1,0:T(8,128)S(1)} fusion(f32[3072,256]{1,0:T(8,128)} %fusion.26, bf16[3072,3072]{1,0:T(8,128)(2,1)S(1)} %bitcast.35, bf16[3072,128]{1,0:T(8,128)(2,1)S(1)} %get-tuple-element.26, bf16[3072,128]{1,0:T(8,128)(2,1)S(1)} %get-tuple-element.25), kind=kOutput, calls=%fused_computation.19 | convolution fusion | flops 4835770368 | bytes 26738688 | tf_op jit(solution)/shard_map/dot_general | solution.py:548
  272.6 30.5 %shard_map.60 = f32[768,128]{1,0:T(8,128)S(1)} custom-call(f32[4,768,128]{2,1,0:T(8,128)S(1)} %bitcast.32), custom_call_target="tpu_custom_call" | custom-call | tf_op jit(solution)/shard_map/pallas_call | solution.py:353
  303.1 0.8 multiply_subtract_fusion
  (34 shorter events, 2.3 us)
Async XLA Ops:
  6.5 63.8 %copy-start.2 = (s32[768]{0:T(1024)S(1)}, s32[768]{0:T(1024)}, u32[]{:S(2)}) copy-start(s32[768]{0:T(1024)} %param.7) | copy-start | bytes 9220
  6.5 63.8 %copy-start.3 = (f32[16]{0:T(128)S(1)}, f32[16]{0:T(128)}, u32[]{:S(2)}) copy-start(f32[16]{0:T(128)} %param.8) | copy-start | bytes 196
  6.5 101.2 %all-gather.2.cloned.1.call-start = ((), (), s32[]{:S(2)}) async-start(), calls=%async_computation | async-start | bytes 1966080 | tf_op jit(solution)/shard_map/all_gather | solution.py:565
  68.7 1.6 copy-start
  107.7 12.6 %slice-start = ((s8[18874368]{0:T(1024)(128)(4,1)}), s8[4194304]{0:T(1024)(128)(4,1)S(1)}, s32[]{:S(2)}) async-start(s8[18874368]{0:T(1024)(128)(4,1)} %bitcast.34), calls=%async_computation.1 | async-start | bytes 8388608
  109.5 10.8 %slice-start.1 = ((s8[18874368]{0:T(1024)(128)(4,1)}), s8[4194304]{0:T(1024)(128)(4,1)S(1)}, s32[]{:S(2)}) async-start(s8[18874368]{0:T(1024)(128)(4,1)} %bitcast.34), calls=%async_computation.2 | async-start | bytes 8388608
  109.6 10.8 %slice-start.2 = ((s8[18874368]{0:T(1024)(128)(4,1)}), s8[4194304]{0:T(1024)(128)(4,1)S(1)}, s32[]{:S(2)}) async-start(s8[18874368]{0:T(1024)(128)(4,1)} %bitcast.34), calls=%async_computation.3 | async-start | bytes 8388608
  109.6 10.8 %slice-start.3 = ((s8[18874368]{0:T(1024)(128)(4,1)}), s8[4194304]{0:T(1024)(128)(4,1)S(1)}, s32[]{:S(2)}) async-start(s8[18874368]{0:T(1024)(128)(4,1)} %bitcast.34), calls=%async_computation.4 | async-start | bytes 8388608
  109.6 11.6 %slice-start.4 = ((s8[18874368]{0:T(1024)(128)(4,1)}), s8[2097152]{0:T(1024)(128)(4,1)S(1)}, s32[]{:S(2)}) async-start(s8[18874368]{0:T(1024)(128)(4,1)} %bitcast.34), calls=%async_computation.5 | async-start | bytes 4194304
  163.1 30.5 %copy-start.1 = (f32[768,128]{1,0:T(8,128)S(1)}, f32[768,128]{1,0:T(8,128)}, u32[]{:S(2)}) copy-start(f32[768,128]{1,0:T(8,128)} %param.6) | copy-start | bytes 1179652
Sparse Core Ops, SparseCore 0:
  70.4 37.2 all-gather.1
